TPU v7x, 32 devices: a whole 2x2x4 slice. The times are simulated.
32 devices in a mesh: rows: 16 (over z, y, core), chan: 2 (over x).
Axes of the slice: x: 2, y: 2, z: 4, core: 2. Of those that a mesh axis runs over, the one named last changes fastest.
Arguments:
- frame_one: bfloat16 [4096, 256], P('rows', 'chan'), may hold values from -6 to 6
- frame_two: bfloat16 [128, 480, 256], P('rows', None, 'chan'), may hold values from -6 to 6
Outputs:
- pyramid: bfloat16 [16, 5040, 4096], P(None, 'chan', 'rows')
All inputs are finite; a program needn't handle non-finite values.
Results may differ from a plain program's by a relative error of at most 0.0016.
Values may be sent and summed in bfloat16 or wider, within the bound.
No kernel may reach another device: no remote copies, remote signals or barrier semaphores. Data moves between devices by JAX's collectives and lax.ppermute only.
A program may use at most 128 MiB of HBM per device.

v0:
```python
import functools

import jax
import jax.numpy as jnp
from jax import lax
from jax.experimental import pallas as pl
from jax.experimental.pallas import tpu as pltpu
from jax.sharding import PartitionSpec as P

LANES = 128
PARAMS = {'LAG': 2, 'F0': 10, 'F1': 0, 'PS0': 2, 'JA': 1, 'JB': 1, 'C0POS': 2, 'R3POS': 0, 'GATE': 30, 'F3': 10, 'F2': 10, 'PE4': 1, 'X00': 10, 'X01': 10, 'C0': 10, 'X10': 10, 'X11': 10, 'C1': 10, 'X20': 10, 'X21': 10, 'C2': 10, 'X30': 10, 'X31': 10, 'C3': 10, 'X40': 10, 'X41': 10, 'C4': 10}


def G(name):
    return PARAMS.get(name, 0)


VMEM_BYTES = 28 * 1024 * 1024


def pool_strip(strip):
    full = strip.astype(jnp.float32)
    rows_n, cols_n, chans = full.shape
    level_one = full.reshape(rows_n // 2, 2, cols_n // 2, 2, chans).mean(axis=(1, 3))
    level_two = level_one.reshape(rows_n // 4, 2, cols_n // 4, 2, chans).mean(axis=(1, 3))
    joined = jnp.concatenate(
        [full.reshape(-1, chans), level_one.reshape(-1, chans), level_two.reshape(-1, chans)],
        axis=0,
    )
    return joined.astype(jnp.bfloat16)


def gather_local(frame_one, frame_two):
    groups = lax.axis_size("chan")
    queries = lax.all_gather(frame_one, "chan", axis=0, tiled=False)
    channels = queries.shape[0] * queries.shape[2]
    factor = 1.0 / jnp.sqrt(jnp.float32(channels))
    pooled = pool_strip(frame_two)
    share = pooled.shape[0] // groups
    traded = lax.all_to_all(
        pooled.reshape(groups, share, pooled.shape[1]), "chan", split_axis=0, concat_axis=0, tiled=True
    )
    gathered = lax.all_gather(traded, "rows", axis=0, tiled=False)
    values = jnp.einsum("skpc,kqc->spq", gathered, queries, preferred_element_type=jnp.float32)
    return (values * factor).astype(jnp.bfloat16)


def pooled_levels(half, sums, sums_two):
    rows_n, cols_n, _ = half.shape
    means = []
    for row in range(rows_n // 2):
        sums[row] = half[2 * row].astype(jnp.float32) + half[2 * row + 1].astype(jnp.float32)
        left = sums[row, pl.ds(0, cols_n // 2, stride=2), :]
        right = sums[row, pl.ds(1, cols_n // 2, stride=2), :]
        means.append((left + right) * 0.25)
    means_two = []
    for row in range(rows_n // 4):
        sums_two[row] = means[2 * row] + means[2 * row + 1]
        left = sums_two[row, pl.ds(0, cols_n // 4, stride=2), :]
        right = sums_two[row, pl.ds(1, cols_n // 4, stride=2), :]
        means_two.append((left + right) * 0.25)
    return jnp.concatenate(means + means_two, axis=0)


def strips_in(refs):
    return [ref.at[index] for ref in refs for index in range(ref.shape[0])]


def extra_kernel(pieces, results, flip, meta, *refs):
    halves = strips_in(refs[:pieces])
    extra, sums, sums_two = refs[-2 - results], *refs[-2:]
    count, cols_n = extra.shape[1], halves[0].shape[1]
    upper = meta[0] == (1 if flip else 0)

    @pl.when(upper)
    def _():
        for index, half in enumerate(halves):
            extra[index] = pooled_levels(half, sums, sums_two).astype(extra.dtype)

    @pl.when(jnp.logical_not(upper))
    def _():
        for index, half in enumerate(halves):
            parts, left, row = [], count, 0
            while left > 0:
                parts.append(half[row].astype(jnp.float32)[: min(left, cols_n)])
                left, row = left - cols_n, row + 1
            extra[index] = jnp.concatenate(parts, axis=0).astype(extra.dtype)


def chunks(segments, step):
    todo, runs = list(segments), []
    while todo:
        run, room = [], step
        while todo and room > 0:
            ref, first, last = todo.pop(0)
            take = min(room, last - first)
            run.append((ref, first, first + take))
            room -= take
            if first + take < last:
                todo.insert(0, (ref, first + take, last))
        runs.append(run)
    return runs


def joined(run):
    parts = [ref[first:last].astype(jnp.float32) for ref, first, last in run]
    return parts[0] if len(parts) == 1 else jnp.concatenate(parts, axis=0)


def corr_kernel(factor, pieces, wide, slots, landing, pins, meta, *refs):
    own, other = strips_in(refs[: pieces[0]]), strips_in(refs[pieces[0] : sum(pieces[:2])])
    refs = refs[sum(pieces[:2]) :]
    came_own, came_other = strips_in(refs[: pieces[2]]), strips_in(refs[pieces[2] : pieces[2] + pieces[3]])
    queries, *refs = refs[pieces[2] + pieces[3] :]
    landed = refs.pop(0) if landing else None
    out, *refs = refs[1 + pins :]
    pair = refs.pop(0) if wide else None
    done, values, sums, sums_two, sems, land_sems = refs
    rows_n, cols_n, _ = own[0].shape
    count, width = came_own[0].shape[0], done.shape[2]
    raw = rows_n * cols_n
    ones = (rows_n // 2) * (cols_n // 2)

    copies = []
    for index, slot in enumerate(landing):
        copies.append(pltpu.make_async_copy(landed.at[index], out.at[meta[slot]], land_sems.at[index]))
        copies[-1].start()

    def times(left):
        return jnp.dot(left, queries[...], preferred_element_type=jnp.float32) * factor

    def store(index, at, part):
        done[index, at : at + part.shape[0]] = part[:, :width].astype(done.dtype)
        if wide:
            pair[index, at : at + part.shape[0]] = part[:, width:].astype(done.dtype)

    for index in range(len(own)):

        def raw_row(row):
            return jnp.concatenate([own[index][row], other[index][row]], axis=1)

        def came_rows():
            return jnp.concatenate([came_own[index][...], came_other[index][...]], axis=1)

        @pl.when(meta[0] == 0)
        def _():
            for row in range(rows_n):
                store(index, row * cols_n, times(raw_row(row)))
            store(index, raw, times(came_rows()))

        @pl.when(meta[0] != 0)
        def _():
            for row in range(count // cols_n, rows_n):
                values[row * cols_n : (row + 1) * cols_n] = times(raw_row(row))
            values[raw : raw + count] = times(came_rows())
            levels = [pooled_levels(half[index], sums, sums_two).astype(done.dtype) for half in (own, other)]
            lower = raw + count
            values[lower : lower + count] = times(jnp.concatenate(levels, axis=1))
            segments = [
                (values, count, raw),
                (values, raw, raw + ones),
                (values, lower, lower + ones),
                (values, raw + ones, raw + count),
                (values, lower + ones, lower + count),
            ]
            step = cols_n // 2
            for at, run in enumerate(chunks(segments, step)):
                store(index, at * step, joined(run))

        copies.append(pltpu.make_async_copy(done.at[index], out.at[meta[slots[index]]], sems.at[index]))
        copies[-1].start()
    for copy in copies:
        copy.wait()


def gate_kernel(*refs):
    pass


def raw_kernel(factor, arrays, wide, landing, meta, *refs):
    own, other = strips_in(refs[:arrays]), strips_in(refs[arrays : 2 * arrays])
    queries, *refs = refs[2 * arrays :]
    landed = refs.pop(0) if landing else None
    _, out, done, *refs = refs
    pair = refs.pop(0) if wide else None
    values, sums, sums_two, land_sems = refs
    rows_n, cols_n, _ = own[0].shape
    count, width = done.shape[1] - rows_n * cols_n, done.shape[2]
    raw = rows_n * cols_n
    ones = (rows_n // 2) * (cols_n // 2)

    copies = []
    for index, slot in enumerate(landing):
        copies.append(pltpu.make_async_copy(landed.at[index], out.at[meta[slot]], land_sems.at[index]))
        copies[-1].start()

    def times(left):
        return jnp.dot(left, queries[...], preferred_element_type=jnp.float32) * factor

    def store(index, at, part):
        done[index, at : at + part.shape[0]] = part[:, :width].astype(done.dtype)
        if wide:
            pair[index, at : at + part.shape[0]] = part[:, width:].astype(done.dtype)

    for index, halves in enumerate(zip(own, other)):

        def raw_row(row):
            return jnp.concatenate([half[row] for half in halves], axis=1)

        @pl.when(meta[0] == 0)
        def _():
            for row in range(rows_n):
                store(index, row * cols_n, times(raw_row(row)))
            store(index, raw, jnp.zeros((count, values.shape[1]), jnp.float32))

        @pl.when(meta[0] != 0)
        def _():
            for row in range(count // cols_n, rows_n):
                values[row * cols_n : (row + 1) * cols_n] = times(raw_row(row))
            levels = [pooled_levels(half, sums, sums_two).astype(done.dtype) for half in halves]
            values[raw : raw + count] = times(jnp.concatenate(levels, axis=1))
            segments = [
                (values, count, raw),
                (values, raw, raw + ones),
                (values, raw, raw + ones),
                (values, raw + ones, raw + count),
                (values, raw + ones, raw + count),
            ]
            step = cols_n // 2
            for at, run in enumerate(chunks(segments, step)):
                store(index, at * step, joined(run))

    for copy in copies:
        copy.wait()


def came_kernel(factor, arrays, wide, late, pins, slots, meta, *refs):
    own, other = strips_in(refs[:arrays]), strips_in(refs[arrays : 2 * arrays])
    queries, *refs = refs[2 * arrays :]
    late_rows = refs.pop(0) if late else None
    refs = refs[2 + late + pins :]
    out, done, *refs = refs
    late_done = refs.pop(0) if late else None
    pair = refs.pop(0) if wide else None
    values, sems = refs
    count, width = own[0].shape[0], done.shape[2]
    raw = done.shape[1] - count
    ones = count * 4 // 5
    copies = []

    def leave(strip):
        copies.append(pltpu.make_async_copy(strip, out.at[meta[slots[len(copies)]]], sems.at[len(copies)]))
        copies[-1].start()

    def merge(strip, part):
        @pl.when(meta[0] == 0)
        def _():
            strip[raw : raw + count] = part.astype(done.dtype)

        @pl.when(meta[0] != 0)
        def _():
            values[...] = part
            at = raw - count
            for first, last, into in ((0, ones, at), (ones, count, at + 2 * ones)):
                start = into // 16 * 16
                end = -(-(into + last - first) // 16) * 16
                parts = [values[first:last]]
                if start < into:
                    parts.insert(0, strip[start : start + 16].astype(jnp.float32)[: into - start])
                over = end - (into + last - first)
                if over:
                    parts.append(strip[end - 16 : end].astype(jnp.float32)[16 - over :])
                strip[start:end] = jnp.concatenate(parts, axis=0).astype(done.dtype)

    if late:
        for index in range(late_done.shape[0]):
            merge(late_done.at[index], late_rows[index].astype(jnp.float32))
            leave(late_done.at[index])
    for index, halves in enumerate(zip(own, other)):
        left = jnp.concatenate([half[...] for half in halves], axis=1)
        part = jnp.dot(left, queries[...], preferred_element_type=jnp.float32) * factor
        if wide:
            pair[index] = part[:, width:].astype(done.dtype)
        merge(done.at[index], part[:, :width])
        leave(done.at[index])
    for copy in copies:
        copy.wait()


def ring_local(frame_one, frame_two):
    rows_axis = lax.axis_size("rows")
    rows_n, cols_n, chans = frame_two.shape
    queries_n = frame_one.shape[0]
    half_rows = rows_n // 2
    raw = half_rows * cols_n
    count = (half_rows // 2) * (cols_n // 2) + (half_rows // 4) * (cols_n // 4)
    factor = float(1.0 / (2 * chans) ** 0.5)
    me, side = lax.axis_index("rows"), lax.axis_index("chan")

    chips = rows_axis // 2
    columns, half_way = chips // 2, chips // 2
    order = [2 * z for z in range(columns)] + [2 * z + 1 for z in reversed(range(columns))]
    ring = [(2 * order[p], 2 * order[(p + 1) % chips]) for p in range(chips)]
    ring += [(2 * order[p] + 1, 2 * order[p - 1] + 1) for p in range(chips)]
    swap = [(r, r ^ 1) for r in range(rows_axis)]
    across = [(0, 1), (1, 0)]

    core, column, line = me % 2, me // 4, (me // 2) % 2
    place = jnp.where(line == 0, column, chips - 1 - column)
    steps = jnp.arange(half_way + 1, dtype=jnp.int32)

    def strips_of(c):
        p = (place + jnp.where(c == 0, -steps, steps)) % chips
        chip = jnp.where(p < columns, 2 * p, 2 * (chips - 1 - p) + 1)
        return [2 * chip + c, 2 * chip + 1 - c]

    meta = jnp.concatenate([side[None], *strips_of(core), *strips_of(1 - core)]).astype(jnp.int32)

    def slots_of(d, other_core):
        first = 1 + (2 * other_core) * (half_way + 1) + d
        return (first,) if d in (0, half_way) else (first, first + half_way + 1)

    in_vmem = pl.BlockSpec(memory_space=pltpu.VMEM)
    anywhere = pl.BlockSpec(memory_space=pl.ANY)
    scalars = pl.BlockSpec(memory_space=pltpu.SMEM)
    out_type = jax.ShapeDtypeStruct((rows_axis, raw + count, queries_n), frame_two.dtype)
    pooling = [
        pltpu.VMEM((half_rows // 2, cols_n, chans), jnp.float32),
        pltpu.VMEM((half_rows // 4, cols_n // 2, chans), jnp.float32),
    ]
    params = pltpu.CompilerParams(vmem_limit_bytes=VMEM_BYTES)
    def modelled(us):
        return pl.CostEstimate(flops=int(us * 10**9) + 1000, bytes_accessed=1000, transcendentals=0)


    def make_extra(out, halves, cost=0, pins=(), flip=False, carry=False):
        strips = sum(half.shape[0] for half in halves)
        handed = () if out is None else (out,)
        carried = tuple(halves) if carry else ()
        aliases = {1 + len(halves): 1} if handed else {}
        aliases.update({1 + index: 2 + index for index in range(len(carried))})
        return pl.pallas_call(
            functools.partial(extra_kernel, len(halves), 2 + len(carried), flip),
            out_shape=(jax.ShapeDtypeStruct((strips, count, chans), frame_two.dtype), out_type)
            + tuple(jax.ShapeDtypeStruct(half.shape, half.dtype) for half in carried),
            in_specs=[scalars] + [in_vmem] * len(halves) + [anywhere] * len(handed + pins),
            out_specs=(in_vmem, anywhere) + (in_vmem,) * len(carried),
            scratch_shapes=pooling,
            input_output_aliases=aliases,
            compiler_params=params,
            cost_estimate=modelled(cost),
            name="extra",
        )(meta, *halves, *handed, *pins)

    def correlate(out, slots, own, other, came_own, came_other, landing=(), landed=None, cost=0, pins=()):
        parts = (own, other, came_own, came_other)
        strips = sum(piece.shape[0] for piece in own)
        operands = [*own, *other, *came_own, *came_other, queries_wide]
        pair_type = jax.ShapeDtypeStruct((strips, raw + count, queries_n), frame_two.dtype)
        return pl.pallas_call(
            functools.partial(corr_kernel, factor, tuple(len(part) for part in parts), True, slots, landing, len(pins)),
            out_shape=(out_type, pair_type),
            in_specs=[scalars] + [in_vmem] * len(operands) + [anywhere] * (1 + bool(landing) + len(pins)),
            out_specs=(anywhere, in_vmem),
            scratch_shapes=[
                pltpu.VMEM((strips, raw + count, queries_n), frame_two.dtype),
                pltpu.VMEM((raw + 2 * count, 2 * queries_n), jnp.float32),
                *pooling,
                pltpu.SemaphoreType.DMA((strips,)),
                pltpu.SemaphoreType.DMA((max(1, len(landing)),)),
            ],
            input_output_aliases={1 + len(operands) + bool(landing): 0},
            compiler_params=params,
            cost_estimate=modelled(cost),
            name="correlate",
        )(meta, *operands, *([landed] if landing else []), out, *pins)

    def product_type(strips, pixels):
        return jax.ShapeDtypeStruct((strips, pixels, queries_n), frame_two.dtype)

    def raw_rows(out, own, other, wide, landing=(), landed=None, cost=0):
        operands = [*own, *other, queries_wide if wide else queries]
        strips = sum(half.shape[0] for half in own)
        return pl.pallas_call(
            functools.partial(raw_kernel, factor, len(own), wide, landing),
            out_shape=(out_type,) + (product_type(strips, raw + count),) * (1 + wide),
            in_specs=[scalars] + [in_vmem] * len(operands) + [anywhere] * (1 + bool(landing)),
            out_specs=(anywhere,) + (in_vmem,) * (1 + wide),
            scratch_shapes=[
                pltpu.VMEM((raw + count, queries_n * (1 + wide)), jnp.float32),
                *pooling,
                pltpu.SemaphoreType.DMA((max(1, len(landing)),)),
            ],
            input_output_aliases={1 + len(operands) + bool(landing): 0},
            compiler_params=params,
            cost_estimate=modelled(cost),
            name="raw_rows",
        )(meta, *operands, *([landed] if landing else []), out)

    def came_rows(out, done, slots, own, other, wide, late=(), cost=0, pins=()):
        operands = [*own, *other, queries_wide if wide else queries, *late[:1]]
        first = 1 + len(operands)
        inout = [out, done, *late[1:]]
        extra_types = (product_type(done.shape[0], count),) if wide else ()
        return pl.pallas_call(
            functools.partial(came_kernel, factor, len(own), wide, len(late) // 2, len(pins), slots),
            out_shape=tuple(jax.ShapeDtypeStruct(array.shape, array.dtype) for array in inout) + extra_types,
            in_specs=[scalars] + [in_vmem] * len(operands) + [anywhere] + [in_vmem] * (len(inout) - 1) + [anywhere] * len(pins),
            out_specs=(anywhere,) + (in_vmem,) * (len(inout) - 1 + wide),
            scratch_shapes=[
                pltpu.VMEM((count, queries_n), jnp.float32),
                pltpu.SemaphoreType.DMA((len(slots),)),
            ],
            input_output_aliases={first + index: index for index in range(len(inout))},
            compiler_params=params,
            cost_estimate=modelled(cost),
            name="came_rows",
        )(meta, *operands, *inout, *pins)

    def gate(out, pins, cost):
        handed = (out, *pins)
        return pl.pallas_call(
            gate_kernel,
            out_shape=tuple(jax.ShapeDtypeStruct(array.shape, array.dtype) for array in handed),
            in_specs=[anywhere] * len(handed),
            out_specs=(anywhere,) * len(handed),
            input_output_aliases={index: index for index in range(len(handed))},
            compiler_params=params,
            cost_estimate=modelled(cost),
            name="gate",
        )(*handed)

    mine = lax.dynamic_slice_in_dim(frame_two, side * half_rows, half_rows, axis=0)[None]
    theirs = lax.dynamic_slice_in_dim(frame_two, (1 - side) * half_rows, half_rows, axis=0)[None]
    if G("XQ"):
        sent = jnp.concatenate([theirs.reshape(raw, chans), frame_one], axis=0)
        got = lax.ppermute(sent, "chan", across)
        partner, queries_other = got[:raw].reshape(theirs.shape), got[raw:]
    else:
        partner = lax.ppermute(theirs, "chan", across)
        queries_other = lax.ppermute(frame_one, "chan", across)
    queries = jnp.concatenate([frame_one.T, queries_other.T], axis=0)
    queries_wide = jnp.concatenate([queries, lax.ppermute(queries, "rows", swap)], axis=1)

    def permute_rows(pairs, pieces):
        return [lax.ppermute(piece, "rows", pairs) for piece in pieces]

    def whole(pieces):
        return pieces if len(pieces) == 1 else [jnp.concatenate(pieces, axis=0)]

    came = {0: ([mine], [partner])}
    moving = [[half, *permute_rows(swap, [half])] for half in (mine, partner)]
    join = [G("JA"), G("JB")]
    for d in range(1, half_way + 1):
        if d == half_way:
            moving = [[pieces[0][:1]] for pieces in moving]
        if d == half_way - 1 and G("BSPL"):
            moving[1] = [moving[1][0][:1], moving[1][0][1:]]
        moving = [
            permute_rows(ring, whole(pieces) if d == join[part] else pieces) for part, pieces in enumerate(moving)
        ]
        came[d] = tuple(moving)
    across_came = {}

    def do_extra(out, d, part, pin=None):
        pins = () if pin is None else tuple(across_came[pin]) if isinstance(pin, tuple) else (pin,)
        across_came[d, 1 - part] = []
        groups = [[piece] for piece in came[d][part]] if part and d == half_way - 1 else [came[d][part]]
        for pieces in groups:
            extra, out = make_extra(out, pieces, G(f"X{d}{part}"), pins)
            across_came[d, 1 - part].append(lax.ppermute(extra, "chan", across))
            pins = ()
        return out

    lag = G("LAG")
    waiting = []

    def landing(now):
        if waiting and waiting[0][0] <= now:
            return waiting.pop(0)[1:]
        return (), None

    def product(out, d, pins=()):
        out, pair = correlate(out, slots_of(d, 0), *came[d], across_came[d, 0], across_came[d, 1], *landing(d), G(f"C{d}"), pins)
        waiting.append((d + lag, slots_of(d, 1), permute_rows(swap, [pair])[0]))
        return out

    out = do_extra(None, 0, 0, partner if G("PINX") else None)
    lacking, out = make_extra(out, [theirs], G("X01"), tuple(across_came[0, 1]) if G("PIN01") else (), flip=True)
    across_came[0, 0] = [lacking]
    if G("C0POS") == 0: out = product(out, 0)
    out = do_extra(out, 1, 0, (0, 1) if G("PIN0") else None)
    if G("C0POS") == 1: out = product(out, 0)
    out = do_extra(out, 1, 1, (1, 1))
    if G("C0POS") == 2: out = product(out, 0)
    for d in range(2, half_way):
        out = do_extra(out, d, 0, (d - 1, 0))
        out = product(out, d - 1)
        out = do_extra(out, d, 1, (d, 1))
    near, far = half_way - 1, half_way

    def swap_one(piece):
        return permute_rows(swap, [piece])[0]

    R3 = G("R3POS")
    def near_raw(out):
        return raw_rows(out, *came[near], True, *landing(near), G("F3"))

    swapped = []

    def far_extra(out, part, pins):
        extra, out, piece = make_extra(out, came[far][part], G(f"X4{part}"), pins, carry=True)
        came[far][part][0] = piece
        across_came[far, 1 - part] = [lax.ppermute(extra, "chan", across)]
        swapped.append(swap_one(piece))
        return out

    if R3 == 0: out, near_done, near_pair = near_raw(out)
    out = far_extra(out, 0, ())
    if R3 == 1: out, near_done, near_pair = near_raw(out)
    out = far_extra(out, 1, (swapped[0],) if G("PS0") == 1 else ())
    near_late = swap_one(near_pair)
    pins = (tuple(across_came[far, 1]) if G("PE4") else ()) + ((swapped[0],) if G("PS0") == 2 else ())

    def far_rows(out):
        return raw_rows(out, [came[far][0][0], swapped[0]], [came[far][1][0], swapped[1]], False, *landing(far), G("F0"))

    def near_came(out):
        return came_rows(out, near_done, slots_of(near, 0), across_came[near, 0], across_came[near, 1], True, cost=G("F2"), pins=pins)

    if G("FAR1"): out, far_done = far_rows(out)
    out, _, near_rows = near_came(out)
    near_rows = swap_one(near_rows)
    if not G("FAR1"): out, far_done = far_rows(out)
    out, own, other = gate(out, [across_came[far, 0][0], across_came[far, 1][0]], G("GATE"))
    slots = slots_of(near, 1) + slots_of(far, 0) + slots_of(far, 1)
    return came_rows(out, far_done, slots, [own, swap_one(own)], [other, swap_one(other)], False, (near_rows, near_late), G("F1"))[0]


def solution(mesh):
    rows_axis, groups = mesh.shape["rows"], mesh.shape["chan"]

    def local(frame_one, frame_two):
        rows_n, cols_n, chans = frame_two.shape
        ring = groups == 2 and rows_axis % 8 == 0 and rows_axis >= 16 and rows_n % 8 == 0 and cols_n % 32 == 0 and chans % LANES == 0
        return (ring_local if ring else gather_local)(frame_one, frame_two)

    in_specs = (P("rows", "chan"), P("rows", None, "chan"))
    out_specs = P(None, "chan", "rows")
    return jax.shard_map(local, mesh=mesh, in_specs=in_specs, out_specs=out_specs, check_vma=False)
```

profile of v0, /device:TPU:0, one launch (start us, length us, event | category | flops | bytes accessed | tf_op | source)
XLA Modules:
  0.0 99.1 jit_solution(5532266728122961580)
XLA Ops:
  0.0 1.2 %dynamic-slice_bitcast_fusion = (bf16[1,4,480,128]{3,2,1,0:T(8,128)(2,1)S(1)}, bf16[1,4,480,128]{3,2,1,0:T(8,128)(2,1)S(1)}) fusion(bf16[8,480,128]{2,1,0:T(8,128)(2,1)} %param.3, s32[]{:T(128)S(6)} %select_n.72, s32[]{:T(128)S(6)} %select_n.71), kind=kLoop, calls=%fused_computation.2 | loop fusion | bytes 1966088 | tf_op jit(solution)/shard_map/broadcast_in_dim | solution.py:434
  1.8 2.6 %collective-permute-start.5 = (bf16[1,4,480,128]{3,2,1,0:T(8,128)(2,1)S(1)}, bf16[1,4,480,128]{3,2,1,0:T(8,128)(2,1)S(1)}, u32[]{:S(2)}, u32[]{:S(2)}) collective-permute-start(bf16[1,4,480,128]{3,2,1,0:T(8,128)(2,1)S(1)} %get-tuple-element.83.refs_0_), channel_id=1, source_target_pairs={{0,1},{1,0},{2,3},{3,2},{4,5},{5,4},{6,7},{7,6},{8,9},{9,8},{10,11... | collective-permute-start | bytes 1474568 | tf_op jit(solution)/shard_map/ppermute | solution.py:440
  4.3 0.9 copy.27
  6.3 2.1 %collective-permute-start.1 = (bf16[2,4,480,128]{3,2,1,0:T(8,128)(2,1)S(1)}, bf16[2,4,480,128]{3,2,1,0:T(8,128)(2,1)S(1)}, u32[]{:S(2)}, u32[]{:S(2)}) collective-permute-start(bf16[2,4,480,128]{3,2,1,0:T(8,128)(2,1)S(1)} %pad_maximum_fusion), channel_id=1, source_target_pairs={{0,8},{8,16},{16,24},{24,28},{28,20},{20,12},{12,4},{4,0},{2,6},{1... | collective-permute-start | bytes 2949128 | tf_op jit(solution)/shard_map/ppermute | solution.py:446
  8.4 8.0 %collective-permute-done.5.refs_1_ = bf16[1,4,480,128]{3,2,1,0:T(8,128)(2,1)S(1)} collective-permute-done((bf16[1,4,480,128]{3,2,1,0:T(8,128)(2,1)S(1)}, bf16[1,4,480,128]{3,2,1,0:T(8,128)(2,1)S(1)}, u32[]{:S(2)}, u32[]{:S(2)}) %collective-permute-start.5) | collective-permute-done | bytes 491552 | tf_op jit(solution)/shard_map/ppermute | solution.py:440
  17.0 1.3 %collective-permute-done.6 = bf16[1,4,480,128]{3,2,1,0:T(8,128)(2,1)S(1)} collective-permute-done((bf16[1,4,480,128]{3,2,1,0:T(8,128)(2,1)S(1)}, bf16[1,4,480,128]{3,2,1,0:T(8,128)(2,1)S(1)}, u32[]{:S(2)}, u32[]{:S(2)}) %collective-permute-start.6) | collective-permute-done | bytes 491552 | tf_op jit(solution)/shard_map/ppermute | solution.py:446
  18.4 2.1 %collective-permute-start.7 = (bf16[2,4,480,128]{3,2,1,0:T(8,128)(2,1)S(1)}, bf16[2,4,480,128]{3,2,1,0:T(8,128)(2,1)S(1)}, u32[]{:S(2)}, u32[]{:S(2)}) collective-permute-start(bf16[2,4,480,128]{3,2,1,0:T(8,128)(2,1)S(1)} %pad_maximum_fusion.1), channel_id=1, source_target_pairs={{0,8},{8,16},{16,24},{24,28},{28,20},{20,12},{12,4},{4,0},{2,6},{1... | collective-permute-start | bytes 2949128 | tf_op jit(solution)/shard_map/ppermute | solution.py:446
  20.5 0.8 extra.12
  21.2 1.8 %collective-permute-start.12 = (bf16[2,600,128]{2,1,0:T(8,128)(2,1)S(1)}, bf16[2,600,128]{2,1,0:T(8,128)(2,1)S(1)}, u32[]{:S(2)}, u32[]{:S(2)}) collective-permute-start(bf16[2,600,128]{2,1,0:T(8,128)(2,1)S(1)} %get-tuple-element.47), channel_id=1, source_target_pairs={{0,1},{1,0},{2,3},{3,2},{4,5},{5,4},{6,7},{7,6},{8,9},{9,8},{10,11... | collective-permute-start | bytes 921608 | tf_op jit(solution)/shard_map/ppermute | solution.py:471
  23.5 0.9 collective-permute-done.11
  24.5 1.6 %collective-permute-start.2 = (bf16[2,4,480,128]{3,2,1,0:T(8,128)(2,1)S(1)}, bf16[2,4,480,128]{3,2,1,0:T(8,128)(2,1)S(1)}, u32[]{:S(2)}, u32[]{:S(2)}) collective-permute-start(bf16[2,4,480,128]{3,2,1,0:T(8,128)(2,1)S(1)} %collective-permute-done.1.refs_0_), channel_id=1, source_target_pairs={{0,8},{8,16},{16,24},{24,28},{28,20},{20,12},{12,4},{4,0},{2,6},{1... | collective-permute-start | bytes 2949128 | tf_op jit(solution)/shard_map/ppermute | solution.py:446
  26.1 5.4 %collective-permute-done.12.refs_2_.refs_3_ = bf16[2,600,128]{2,1,0:T(8,128)(2,1)S(1)} collective-permute-done((bf16[2,600,128]{2,1,0:T(8,128)(2,1)S(1)}, bf16[2,600,128]{2,1,0:T(8,128)(2,1)S(1)}, u32[]{:S(2)}, u32[]{:S(2)}) %collective-permute-start.12) | collective-permute-done | bytes 307232 | tf_op jit(solution)/shard_map/ppermute | solution.py:471
  31.5 1.0 %collective-permute-done.7.refs_0_.refs_1_ = bf16[2,4,480,128]{3,2,1,0:T(8,128)(2,1)S(1)} collective-permute-done((bf16[2,4,480,128]{3,2,1,0:T(8,128)(2,1)S(1)}, bf16[2,4,480,128]{3,2,1,0:T(8,128)(2,1)S(1)}, u32[]{:S(2)}, u32[]{:S(2)}) %collective-permute-start.7) | collective-permute-done | bytes 983072 | tf_op jit(solution)/shard_map/ppermute | solution.py:446
  32.5 0.8 extra.13
  33.3 1.8 %collective-permute-start.13 = (bf16[2,600,128]{2,1,0:T(8,128)(2,1)S(1)}, bf16[2,600,128]{2,1,0:T(8,128)(2,1)S(1)}, u32[]{:S(2)}, u32[]{:S(2)}) collective-permute-start(bf16[2,600,128]{2,1,0:T(8,128)(2,1)S(1)} %get-tuple-element.48), channel_id=1, source_target_pairs={{0,1},{1,0},{2,3},{3,2},{4,5},{5,4},{6,7},{7,6},{8,9},{9,8},{10,11... | collective-permute-start | bytes 921608 | tf_op jit(solution)/shard_map/ppermute | solution.py:471
  35.1 2.5 %correlate.3 = (bf16[16,2520,256]{2,1,0:T(8,128)(2,1)}, bf16[1,2520,256]{2,1,0:T(8,128)(2,1)S(1)}) custom-call(s32[21]{0:T(128)S(1)} %concatenate.15.meta, bf16[1,4,480,128]{3,2,1,0:T(8,128)(2,1)S(1)} %get-tuple-element.84.refs_0_, bf16[1,4,480,128]{3,2,1,0:T(8,128)(2,1)S(1)} %collective-permute-done.5.refs_1_, ...), custom_call_target="tpu_custom_call", output_to_operand_aliasing={{0}: (6, {})} | custom-call | flops 10000001024 | bytes 1000 | tf_op jit(solution)/shard_map/correlate/pallas_call | solution.py:360
  37.7 1.6 %collective-permute-start.8 = (bf16[2,4,480,128]{3,2,1,0:T(8,128)(2,1)S(1)}, bf16[2,4,480,128]{3,2,1,0:T(8,128)(2,1)S(1)}, u32[]{:S(2)}, u32[]{:S(2)}) collective-permute-start(bf16[2,4,480,128]{3,2,1,0:T(8,128)(2,1)S(1)} %collective-permute-done.7.refs_0_.refs_1_), channel_id=1, source_target_pairs={{0,8},{8,16},{16,24},{24,28},{28,20},{20,12},{12,4},{4,0},{2,6},{1... | collective-permute-start | bytes 2949128 | tf_op jit(solution)/shard_map/ppermute | solution.py:446
  39.3 2.8 %collective-permute-done.13.refs_2_ = bf16[2,600,128]{2,1,0:T(8,128)(2,1)S(1)} collective-permute-done((bf16[2,600,128]{2,1,0:T(8,128)(2,1)S(1)}, bf16[2,600,128]{2,1,0:T(8,128)(2,1)S(1)}, u32[]{:S(2)}, u32[]{:S(2)}) %collective-permute-start.13) | collective-permute-done | bytes 307232 | tf_op jit(solution)/shard_map/ppermute | solution.py:471
  42.1 0.9 collective-permute-done.2.refs_0_
  43.0 0.8 extra.14
  43.8 1.8 %collective-permute-start.16 = (bf16[2,600,128]{2,1,0:T(8,128)(2,1)S(1)}, bf16[2,600,128]{2,1,0:T(8,128)(2,1)S(1)}, u32[]{:S(2)}, u32[]{:S(2)}) collective-permute-start(bf16[2,600,128]{2,1,0:T(8,128)(2,1)S(1)} %get-tuple-element.56), channel_id=1, source_target_pairs={{0,1},{1,0},{2,3},{3,2},{4,5},{5,4},{6,7},{7,6},{8,9},{9,8},{10,11... | collective-permute-start | bytes 921608 | tf_op jit(solution)/shard_map/ppermute | solution.py:471
  45.7 1.6 %collective-permute-start.3 = (bf16[2,4,480,128]{3,2,1,0:T(8,128)(2,1)S(1)}, bf16[2,4,480,128]{3,2,1,0:T(8,128)(2,1)S(1)}, u32[]{:S(2)}, u32[]{:S(2)}) collective-permute-start(bf16[2,4,480,128]{3,2,1,0:T(8,128)(2,1)S(1)} %collective-permute-done.2.refs_0_), channel_id=1, source_target_pairs={{0,8},{8,16},{16,24},{24,28},{28,20},{20,12},{12,4},{4,0},{2,6},{1... | collective-permute-start | bytes 2949128 | tf_op jit(solution)/shard_map/ppermute | solution.py:446
  47.2 3.3 %correlate.4 = (bf16[16,2520,256]{2,1,0:T(8,128)(2,1)}, bf16[2,2520,256]{2,1,0:T(8,128)(2,1)S(1)}) custom-call(s32[21]{0:T(128)S(1)} %concatenate.15.meta, bf16[2,4,480,128]{3,2,1,0:T(8,128)(2,1)S(1)} %collective-permute-done.1.refs_0_, bf16[2,4,480,128]{3,2,1,0:T(8,128)(2,1)S(1)} %collective-permute-done.7.refs_0_.refs_1_, ...), custom_call_target="tpu_custom_call", output_to_operand_aliasing={{0}: (6, {})} | custom-call | flops 10000001024 | bytes 1000 | tf_op jit(solution)/shard_map/correlate/pallas_call | solution.py:360
  50.6 2.1 %collective-permute-done.16.refs_2_.refs_3_ = bf16[2,600,128]{2,1,0:T(8,128)(2,1)S(1)} collective-permute-done((bf16[2,600,128]{2,1,0:T(8,128)(2,1)S(1)}, bf16[2,600,128]{2,1,0:T(8,128)(2,1)S(1)}, u32[]{:S(2)}, u32[]{:S(2)}) %collective-permute-start.16) | collective-permute-done | bytes 307232 | tf_op jit(solution)/shard_map/ppermute | solution.py:471
  52.6 0.9 collective-permute-done.8.refs_0_.refs_1_
  53.6 0.8 extra.15
  54.4 1.8 %collective-permute-start.17 = (bf16[2,600,128]{2,1,0:T(8,128)(2,1)S(1)}, bf16[2,600,128]{2,1,0:T(8,128)(2,1)S(1)}, u32[]{:S(2)}, u32[]{:S(2)}) collective-permute-start(bf16[2,600,128]{2,1,0:T(8,128)(2,1)S(1)} %get-tuple-element.57), channel_id=1, source_target_pairs={{0,1},{1,0},{2,3},{3,2},{4,5},{5,4},{6,7},{7,6},{8,9},{9,8},{10,11... | collective-permute-start | bytes 921608 | tf_op jit(solution)/shard_map/ppermute | solution.py:471
  56.2 1.6 %collective-permute-start.9 = (bf16[2,4,480,128]{3,2,1,0:T(8,128)(2,1)S(1)}, bf16[2,4,480,128]{3,2,1,0:T(8,128)(2,1)S(1)}, u32[]{:S(2)}, u32[]{:S(2)}) collective-permute-start(bf16[2,4,480,128]{3,2,1,0:T(8,128)(2,1)S(1)} %collective-permute-done.8.refs_0_.refs_1_), channel_id=1, source_target_pairs={{0,8},{8,16},{16,24},{24,28},{28,20},{20,12},{12,4},{4,0},{2,6},{1... | collective-permute-start | bytes 2949128 | tf_op jit(solution)/shard_map/ppermute | solution.py:446
  57.8 5.4 %collective-permute-done.17.refs_2_ = bf16[2,600,128]{2,1,0:T(8,128)(2,1)S(1)} collective-permute-done((bf16[2,600,128]{2,1,0:T(8,128)(2,1)S(1)}, bf16[2,600,128]{2,1,0:T(8,128)(2,1)S(1)}, u32[]{:S(2)}, u32[]{:S(2)}) %collective-permute-start.17) | collective-permute-done | bytes 307232 | tf_op jit(solution)/shard_map/ppermute | solution.py:471
  63.2 0.9 collective-permute-done.3.refs_0_
  64.1 0.8 extra.16
  64.9 1.8 %collective-permute-start.19 = (bf16[2,600,128]{2,1,0:T(8,128)(2,1)S(1)}, bf16[2,600,128]{2,1,0:T(8,128)(2,1)S(1)}, u32[]{:S(2)}, u32[]{:S(2)}) collective-permute-start(bf16[2,600,128]{2,1,0:T(8,128)(2,1)S(1)} %get-tuple-element.62), channel_id=1, source_target_pairs={{0,1},{1,0},{2,3},{3,2},{4,5},{5,4},{6,7},{7,6},{8,9},{9,8},{10,11... | collective-permute-start | bytes 921608 | tf_op jit(solution)/shard_map/ppermute | solution.py:471
  66.8 1.6 %collective-permute-start.4 = (bf16[1,4,480,128]{3,2,1,0:T(8,128)(2,1)S(1)}, bf16[1,4,480,128]{3,2,1,0:T(8,128)(2,1)S(1)}, u32[]{:S(2)}, u32[]{:S(2)}) collective-permute-start(bf16[1,4,480,128]{3,2,1,0:T(8,128)(2,1)S(1)} %slice.8), channel_id=1, source_target_pairs={{0,8},{8,16},{16,24},{24,28},{28,20},{20,12},{12,4},{4,0},{2,6},{1... | collective-permute-start | bytes 1474568 | tf_op jit(solution)/shard_map/ppermute | solution.py:446
  68.4 3.3 %correlate.5 = (bf16[16,2520,256]{2,1,0:T(8,128)(2,1)}, bf16[2,2520,256]{2,1,0:T(8,128)(2,1)S(1)}) custom-call(s32[21]{0:T(128)S(1)} %concatenate.15.meta, bf16[2,4,480,128]{3,2,1,0:T(8,128)(2,1)S(1)} %collective-permute-done.2.refs_0_, bf16[2,4,480,128]{3,2,1,0:T(8,128)(2,1)S(1)} %collective-permute-done.8.refs_0_.refs_1_, ...), custom_call_target="tpu_custom_call", output_to_operand_aliasing={{0}: (7, {})} | custom-call | flops 10000001024 | bytes 1000 | tf_op jit(solution)/shard_map/correlate/pallas_call | solution.py:360
  71.8 2.8 %collective-permute-done.9.refs_0_.refs_1_ = bf16[2,4,480,128]{3,2,1,0:T(8,128)(2,1)S(1)} collective-permute-done((bf16[2,4,480,128]{3,2,1,0:T(8,128)(2,1)S(1)}, bf16[2,4,480,128]{3,2,1,0:T(8,128)(2,1)S(1)}, u32[]{:S(2)}, u32[]{:S(2)}) %collective-permute-start.9) | collective-permute-done | bytes 983072 | tf_op jit(solution)/shard_map/ppermute | solution.py:446
  74.7 2.1 %collective-permute-start.21 = (bf16[1,4,480,128]{3,2,1,0:T(8,128)(2,1)S(1)}, bf16[1,4,480,128]{3,2,1,0:T(8,128)(2,1)S(1)}, u32[]{:S(2)}, u32[]{:S(2)}) collective-permute-start(bf16[1,4,480,128]{3,2,1,0:T(8,128)(2,1)S(1)} %slice.9), channel_id=1, source_target_pairs={{0,8},{8,16},{16,24},{24,28},{28,20},{20,12},{12,4},{4,0},{2,6},{1... | collective-permute-start | bytes 1474568 | tf_op jit(solution)/shard_map/ppermute | solution.py:446
  76.8 1.0 extra.17
  77.7 1.4 %collective-permute-start.24 = (bf16[2,600,128]{2,1,0:T(8,128)(2,1)S(1)}, bf16[2,600,128]{2,1,0:T(8,128)(2,1)S(1)}, u32[]{:S(2)}, u32[]{:S(2)}) collective-permute-start(bf16[2,600,128]{2,1,0:T(8,128)(2,1)S(1)} %get-tuple-element.69), channel_id=1, source_target_pairs={{0,1},{1,0},{2,3},{3,2},{4,5},{5,4},{6,7},{7,6},{8,9},{9,8},{10,11... | collective-permute-start | bytes 921608 | tf_op jit(solution)/shard_map/ppermute | solution.py:471
  79.1 2.0 %raw_rows.2 = (bf16[16,2520,256]{2,1,0:T(8,128)(2,1)}, bf16[2,2520,256]{2,1,0:T(8,128)(2,1)S(1)}, bf16[2,2520,256]{2,1,0:T(8,128)(2,1)S(1)}) custom-call(s32[21]{0:T(128)S(1)} %concatenate.15.meta, bf16[2,4,480,128]{3,2,1,0:T(8,128)(2,1)S(1)} %collective-permute-done.3.refs_0_, ...), custom_call_target="tpu_custom_call", output_to_operand_aliasing={{0}: (5, {})} | custom-call | flops 10000001024 | bytes 1000 | tf_op jit(solution)/shard_map/raw_rows/pallas_call | solution.py:384
  81.9 0.9 collective-permute-start.25
  82.9 2.3 %collective-permute-done.21.refs_0_ = bf16[1,4,480,128]{3,2,1,0:T(8,128)(2,1)S(1)} collective-permute-done((bf16[1,4,480,128]{3,2,1,0:T(8,128)(2,1)S(1)}, bf16[1,4,480,128]{3,2,1,0:T(8,128)(2,1)S(1)}, u32[]{:S(2)}, u32[]{:S(2)}) %collective-permute-start.21) | collective-permute-done | bytes 491552 | tf_op jit(solution)/shard_map/ppermute | solution.py:446
  85.9 0.8 collective-permute-done.24.refs_0_
  86.7 1.8 %collective-permute-start.26 = (bf16[1,600,128]{2,1,0:T(8,128)(2,1)S(1)}, bf16[1,600,128]{2,1,0:T(8,128)(2,1)S(1)}, u32[]{:S(2)}, u32[]{:S(2)}) collective-permute-start(bf16[1,600,128]{2,1,0:T(8,128)(2,1)S(1)} %get-tuple-element.75), channel_id=1, source_target_pairs={{0,1},{1,0},{2,3},{3,2},{4,5},{5,4},{6,7},{7,6},{8,9},{9,8},{10,11... | collective-permute-start | bytes 460808 | tf_op jit(solution)/shard_map/ppermute | solution.py:514
  88.5 0.7 collective-permute-done.25.refs_5_.refs_2_
  89.2 2.4 %came_rows.2 = (bf16[16,2520,256]{2,1,0:T(8,128)(2,1)}, bf16[2,2520,256]{2,1,0:T(8,128)(2,1)S(1)}, bf16[2,600,256]{2,1,0:T(8,128)(2,1)S(1)}) custom-call(s32[21]{0:T(128)S(1)} %concatenate.15.meta, bf16[2,600,128]{2,1,0:T(8,128)(2,1)S(1)} %collective-permute-done.24.refs_0_, ...), custom_call_target="tpu_custom_call", output_to_operand_aliasing={{0}: (4, {}), {1}: (5, {})} | custom-call | flops 10000001024 | bytes 1000 | tf_op jit(solution)/shard_map/came_rows/pallas_call | solution.py:405
  92.2 2.0 %raw_rows.3 = (bf16[16,2520,256]{2,1,0:T(8,128)(2,1)}, bf16[2,2520,256]{2,1,0:T(8,128)(2,1)S(1)}) custom-call(s32[21]{0:T(128)S(1)} %concatenate.15.meta, bf16[1,4,480,128]{3,2,1,0:T(8,128)(2,1)S(1)} %get-tuple-element.65.refs_0_, bf16[1,4,480,128]{3,2,1,0:T(8,128)(2,1)S(1)} %collective-permute-done.20.refs_6_.refs_1_, ...), custom_call_target="tpu_custom_call", output_to_operand_aliasing={{0}: (7, {})} | custom-call | flops 10000001024 | bytes 1000 | tf_op jit(solution)/shard_map/raw_rows/pallas_call | solution.py:384
  94.9 0.8 collective-permute-done.27.refs_1_
  96.0 2.9 %came_rows.3 = (bf16[16,2520,256]{2,1,0:T(8,128)(2,1)}, bf16[2,2520,256]{2,1,0:T(8,128)(2,1)S(1)}, bf16[2,2520,256]{2,1,0:T(8,128)(2,1)S(1)}) custom-call(s32[21]{0:T(128)S(1)} %concatenate.15.meta, bf16[1,600,128]{2,1,0:T(8,128)(2,1)S(1)} %get-tuple-element.76.refs_0_, ...), custom_call_target="tpu_custom_call", output_to_operand_aliasing={{0}: (7, {}), {1}: (8, {}), {2}: (9, {})} | custom-call | flops 1000 | bytes 1000 | tf_op jit(solution)/shard_map/came_rows/pallas_call | solution.py:405
  (43 shorter events, 5.8 us)
Async XLA Ops:
  1.2 5.0 %collective-permute-start = (bf16[1,4,480,128]{3,2,1,0:T(8,128)(2,1)S(1)}, bf16[1,4,480,128]{3,2,1,0:T(8,128)(2,1)S(1)}, u32[]{:S(2)}, u32[]{:S(2)}) collective-permute-start(bf16[1,4,480,128]{3,2,1,0:T(8,128)(2,1)S(1)} %get-tuple-element.84.refs_0_), channel_id=1, source_target_pairs={{0,2},{2,0},{4,6},{6,4},{8,10},{10,8},{12,14},{14,12},{16,18},{18,... | collective-permute-start | bytes 1474568 | tf_op jit(solution)/shard_map/ppermute | solution.py:446
  1.8 14.6 %collective-permute-start.5 = (bf16[1,4,480,128]{3,2,1,0:T(8,128)(2,1)S(1)}, bf16[1,4,480,128]{3,2,1,0:T(8,128)(2,1)S(1)}, u32[]{:S(2)}, u32[]{:S(2)}) collective-permute-start(bf16[1,4,480,128]{3,2,1,0:T(8,128)(2,1)S(1)} %get-tuple-element.83.refs_0_), channel_id=1, source_target_pairs={{0,1},{1,0},{2,3},{3,2},{4,5},{5,4},{6,7},{7,6},{8,9},{9,8},{10,11... | collective-permute-start | bytes 1474568 | tf_op jit(solution)/shard_map/ppermute | solution.py:440
  5.3 17.7 %collective-permute-start.10 = (bf16[256,128]{0,1:T(8,128)(2,1)S(1)}, bf16[256,128]{0,1:T(8,128)(2,1)S(1)}, u32[]{:S(2)}, u32[]{:S(2)}) collective-permute-start(bf16[256,128]{0,1:T(8,128)(2,1)S(1)} %copy.27), channel_id=1, source_target_pairs={{0,1},{1,0},{2,3},{3,2},{4,5},{5,4},{6,7},{7,6},{8,9},{9,8},{10,11... | collective-permute-start | bytes 196616 | tf_op jit(solution)/shard_map/ppermute | solution.py:441
  6.3 14.1 %collective-permute-start.1 = (bf16[2,4,480,128]{3,2,1,0:T(8,128)(2,1)S(1)}, bf16[2,4,480,128]{3,2,1,0:T(8,128)(2,1)S(1)}, u32[]{:S(2)}, u32[]{:S(2)}) collective-permute-start(bf16[2,4,480,128]{3,2,1,0:T(8,128)(2,1)S(1)} %pad_maximum_fusion), channel_id=1, source_target_pairs={{0,8},{8,16},{16,24},{24,28},{28,20},{20,12},{12,4},{4,0},{2,6},{1... | collective-permute-start | bytes 2949128 | tf_op jit(solution)/shard_map/ppermute | solution.py:446
  16.4 1.9 %collective-permute-start.6 = (bf16[1,4,480,128]{3,2,1,0:T(8,128)(2,1)S(1)}, bf16[1,4,480,128]{3,2,1,0:T(8,128)(2,1)S(1)}, u32[]{:S(2)}, u32[]{:S(2)}) collective-permute-start(bf16[1,4,480,128]{3,2,1,0:T(8,128)(2,1)S(1)} %collective-permute-done.5.refs_1_), channel_id=1, source_target_pairs={{0,2},{2,0},{4,6},{6,4},{8,10},{10,8},{12,14},{14,12},{16,18},{18,... | collective-permute-start | bytes 1474568 | tf_op jit(solution)/shard_map/ppermute | solution.py:446
  18.4 14.1 %collective-permute-start.7 = (bf16[2,4,480,128]{3,2,1,0:T(8,128)(2,1)S(1)}, bf16[2,4,480,128]{3,2,1,0:T(8,128)(2,1)S(1)}, u32[]{:S(2)}, u32[]{:S(2)}) collective-permute-start(bf16[2,4,480,128]{3,2,1,0:T(8,128)(2,1)S(1)} %pad_maximum_fusion.1), channel_id=1, source_target_pairs={{0,8},{8,16},{16,24},{24,28},{28,20},{20,12},{12,4},{4,0},{2,6},{1... | collective-permute-start | bytes 2949128 | tf_op jit(solution)/shard_map/ppermute | solution.py:446
  21.2 10.2 %collective-permute-start.12 = (bf16[2,600,128]{2,1,0:T(8,128)(2,1)S(1)}, bf16[2,600,128]{2,1,0:T(8,128)(2,1)S(1)}, u32[]{:S(2)}, u32[]{:S(2)}) collective-permute-start(bf16[2,600,128]{2,1,0:T(8,128)(2,1)S(1)} %get-tuple-element.47), channel_id=1, source_target_pairs={{0,1},{1,0},{2,3},{3,2},{4,5},{5,4},{6,7},{7,6},{8,9},{9,8},{10,11... | collective-permute-start | bytes 921608 | tf_op jit(solution)/shard_map/ppermute | solution.py:471
  23.0 1.4 %collective-permute-start.11 = (bf16[256,256]{1,0:T(8,128)(2,1)S(1)}, bf16[256,256]{1,0:T(8,128)(2,1)S(1)}, u32[]{:S(2)}, u32[]{:S(2)}) collective-permute-start(bf16[256,256]{1,0:T(8,128)(2,1)S(1)} %pad_maximum_fusion.3.refs_4_), channel_id=1, source_target_pairs={{0,2},{2,0},{4,6},{6,4},{8,10},{10,8},{12,14},{14,12},{16,18},{18,... | collective-permute-start | bytes 393224 | tf_op jit(solution)/shard_map/ppermute | solution.py:443
  23.1 12.0 %collective-permute-start.14 = (bf16[1,600,128]{2,1,0:T(8,128)(2,1)S(1)}, bf16[1,600,128]{2,1,0:T(8,128)(2,1)S(1)}, u32[]{:S(2)}, u32[]{:S(2)}) collective-permute-start(bf16[1,600,128]{2,1,0:T(8,128)(2,1)S(1)} %get-tuple-element.50), channel_id=1, source_target_pairs={{0,1},{1,0},{2,3},{3,2},{4,5},{5,4},{6,7},{7,6},{8,9},{9,8},{10,11... | collective-permute-start | bytes 460808 | tf_op jit(solution)/shard_map/ppermute | solution.py:471
  24.5 18.6 %collective-permute-start.2 = (bf16[2,4,480,128]{3,2,1,0:T(8,128)(2,1)S(1)}, bf16[2,4,480,128]{3,2,1,0:T(8,128)(2,1)S(1)}, u32[]{:S(2)}, u32[]{:S(2)}) collective-permute-start(bf16[2,4,480,128]{3,2,1,0:T(8,128)(2,1)S(1)} %collective-permute-done.1.refs_0_), channel_id=1, source_target_pairs={{0,8},{8,16},{16,24},{24,28},{28,20},{20,12},{12,4},{4,0},{2,6},{1... | collective-permute-start | bytes 2949128 | tf_op jit(solution)/shard_map/ppermute | solution.py:446
  33.3 8.8 %collective-permute-start.13 = (bf16[2,600,128]{2,1,0:T(8,128)(2,1)S(1)}, bf16[2,600,128]{2,1,0:T(8,128)(2,1)S(1)}, u32[]{:S(2)}, u32[]{:S(2)}) collective-permute-start(bf16[2,600,128]{2,1,0:T(8,128)(2,1)S(1)} %get-tuple-element.48), channel_id=1, source_target_pairs={{0,1},{1,0},{2,3},{3,2},{4,5},{5,4},{6,7},{7,6},{8,9},{9,8},{10,11... | collective-permute-start | bytes 921608 | tf_op jit(solution)/shard_map/ppermute | solution.py:471
  37.6 30.8 %collective-permute-start.18 = (bf16[1,2520,256]{2,1,0:T(8,128)(2,1)S(1)}, bf16[1,2520,256]{2,1,0:T(8,128)(2,1)S(1)}, u32[]{:S(2)}, u32[]{:S(2)}) collective-permute-start(bf16[1,2520,256]{2,1,0:T(8,128)(2,1)S(1)} %get-tuple-element.58), channel_id=1, source_target_pairs={{0,2},{2,0},{4,6},{6,4},{8,10},{10,8},{12,14},{14,12},{16,18},{18,... | collective-permute-start | bytes 3870728 | tf_op jit(solution)/shard_map/ppermute | solution.py:446
  37.7 15.9 %collective-permute-start.8 = (bf16[2,4,480,128]{3,2,1,0:T(8,128)(2,1)S(1)}, bf16[2,4,480,128]{3,2,1,0:T(8,128)(2,1)S(1)}, u32[]{:S(2)}, u32[]{:S(2)}) collective-permute-start(bf16[2,4,480,128]{3,2,1,0:T(8,128)(2,1)S(1)} %collective-permute-done.7.refs_0_.refs_1_), channel_id=1, source_target_pairs={{0,8},{8,16},{16,24},{24,28},{28,20},{20,12},{12,4},{4,0},{2,6},{1... | collective-permute-start | bytes 2949128 | tf_op jit(solution)/shard_map/ppermute | solution.py:446
  43.8 8.8 %collective-permute-start.16 = (bf16[2,600,128]{2,1,0:T(8,128)(2,1)S(1)}, bf16[2,600,128]{2,1,0:T(8,128)(2,1)S(1)}, u32[]{:S(2)}, u32[]{:S(2)}) collective-permute-start(bf16[2,600,128]{2,1,0:T(8,128)(2,1)S(1)} %get-tuple-element.56), channel_id=1, source_target_pairs={{0,1},{1,0},{2,3},{3,2},{4,5},{5,4},{6,7},{7,6},{8,9},{9,8},{10,11... | collective-permute-start | bytes 921608 | tf_op jit(solution)/shard_map/ppermute | solution.py:471
  45.7 18.4 %collective-permute-start.3 = (bf16[2,4,480,128]{3,2,1,0:T(8,128)(2,1)S(1)}, bf16[2,4,480,128]{3,2,1,0:T(8,128)(2,1)S(1)}, u32[]{:S(2)}, u32[]{:S(2)}) collective-permute-start(bf16[2,4,480,128]{3,2,1,0:T(8,128)(2,1)S(1)} %collective-permute-done.2.refs_0_), channel_id=1, source_target_pairs={{0,8},{8,16},{16,24},{24,28},{28,20},{20,12},{12,4},{4,0},{2,6},{1... | collective-permute-start | bytes 2949128 | tf_op jit(solution)/shard_map/ppermute | solution.py:446
  54.4 8.8 %collective-permute-start.17 = (bf16[2,600,128]{2,1,0:T(8,128)(2,1)S(1)}, bf16[2,600,128]{2,1,0:T(8,128)(2,1)S(1)}, u32[]{:S(2)}, u32[]{:S(2)}) collective-permute-start(bf16[2,600,128]{2,1,0:T(8,128)(2,1)S(1)} %get-tuple-element.57), channel_id=1, source_target_pairs={{0,1},{1,0},{2,3},{3,2},{4,5},{5,4},{6,7},{7,6},{8,9},{9,8},{10,11... | collective-permute-start | bytes 921608 | tf_op jit(solution)/shard_map/ppermute | solution.py:471
  56.2 22.9 %collective-permute-start.15 = (bf16[2,2520,256]{2,1,0:T(8,128)(2,1)S(1)}, bf16[2,2520,256]{2,1,0:T(8,128)(2,1)S(1)}, u32[]{:S(2)}, u32[]{:S(2)}) collective-permute-start(bf16[2,2520,256]{2,1,0:T(8,128)(2,1)S(1)} %get-tuple-element.54), channel_id=1, source_target_pairs={{0,2},{2,0},{4,6},{6,4},{8,10},{10,8},{12,14},{14,12},{16,18},{18,... | collective-permute-start | bytes 7741448 | tf_op jit(solution)/shard_map/ppermute | solution.py:446
  56.2 18.4 %collective-permute-start.9 = (bf16[2,4,480,128]{3,2,1,0:T(8,128)(2,1)S(1)}, bf16[2,4,480,128]{3,2,1,0:T(8,128)(2,1)S(1)}, u32[]{:S(2)}, u32[]{:S(2)}) collective-permute-start(bf16[2,4,480,128]{3,2,1,0:T(8,128)(2,1)S(1)} %collective-permute-done.8.refs_0_.refs_1_), channel_id=1, source_target_pairs={{0,8},{8,16},{16,24},{24,28},{28,20},{20,12},{12,4},{4,0},{2,6},{1... | collective-permute-start | bytes 2949128 | tf_op jit(solution)/shard_map/ppermute | solution.py:446
  64.9 11.9 %collective-permute-start.19 = (bf16[2,600,128]{2,1,0:T(8,128)(2,1)S(1)}, bf16[2,600,128]{2,1,0:T(8,128)(2,1)S(1)}, u32[]{:S(2)}, u32[]{:S(2)}) collective-permute-start(bf16[2,600,128]{2,1,0:T(8,128)(2,1)S(1)} %get-tuple-element.62), channel_id=1, source_target_pairs={{0,1},{1,0},{2,3},{3,2},{4,5},{5,4},{6,7},{7,6},{8,9},{9,8},{10,11... | collective-permute-start | bytes 921608 | tf_op jit(solution)/shard_map/ppermute | solution.py:471
  66.8 14.4 %collective-permute-start.4 = (bf16[1,4,480,128]{3,2,1,0:T(8,128)(2,1)S(1)}, bf16[1,4,480,128]{3,2,1,0:T(8,128)(2,1)S(1)}, u32[]{:S(2)}, u32[]{:S(2)}) collective-permute-start(bf16[1,4,480,128]{3,2,1,0:T(8,128)(2,1)S(1)} %slice.8), channel_id=1, source_target_pairs={{0,8},{8,16},{16,24},{24,28},{28,20},{20,12},{12,4},{4,0},{2,6},{1... | collective-permute-start | bytes 1474568 | tf_op jit(solution)/shard_map/ppermute | solution.py:446
  71.7 20.5 %collective-permute-start.23 = (bf16[2,2520,256]{2,1,0:T(8,128)(2,1)S(1)}, bf16[2,2520,256]{2,1,0:T(8,128)(2,1)S(1)}, u32[]{:S(2)}, u32[]{:S(2)}) collective-permute-start(bf16[2,2520,256]{2,1,0:T(8,128)(2,1)S(1)} %get-tuple-element.68), channel_id=1, source_target_pairs={{0,2},{2,0},{4,6},{6,4},{8,10},{10,8},{12,14},{14,12},{16,18},{18,... | collective-permute-start | bytes 7741448 | tf_op jit(solution)/shard_map/ppermute | solution.py:446
  74.7 10.5 %collective-permute-start.21 = (bf16[1,4,480,128]{3,2,1,0:T(8,128)(2,1)S(1)}, bf16[1,4,480,128]{3,2,1,0:T(8,128)(2,1)S(1)}, u32[]{:S(2)}, u32[]{:S(2)}) collective-permute-start(bf16[1,4,480,128]{3,2,1,0:T(8,128)(2,1)S(1)} %slice.9), channel_id=1, source_target_pairs={{0,8},{8,16},{16,24},{24,28},{28,20},{20,12},{12,4},{4,0},{2,6},{1... | collective-permute-start | bytes 1474568 | tf_op jit(solution)/shard_map/ppermute | solution.py:446
  77.7 9.0 %collective-permute-start.24 = (bf16[2,600,128]{2,1,0:T(8,128)(2,1)S(1)}, bf16[2,600,128]{2,1,0:T(8,128)(2,1)S(1)}, u32[]{:S(2)}, u32[]{:S(2)}) collective-permute-start(bf16[2,600,128]{2,1,0:T(8,128)(2,1)S(1)} %get-tuple-element.69), channel_id=1, source_target_pairs={{0,1},{1,0},{2,3},{3,2},{4,5},{5,4},{6,7},{7,6},{8,9},{9,8},{10,11... | collective-permute-start | bytes 921608 | tf_op jit(solution)/shard_map/ppermute | solution.py:471
  81.8 7.4 %collective-permute-start.20 = (bf16[1,4,480,128]{3,2,1,0:T(8,128)(2,1)S(1)}, bf16[1,4,480,128]{3,2,1,0:T(8,128)(2,1)S(1)}, u32[]{:S(2)}, u32[]{:S(2)}) collective-permute-start(bf16[1,4,480,128]{3,2,1,0:T(8,128)(2,1)S(1)} %get-tuple-element.65.refs_0_), channel_id=1, source_target_pairs={{0,2},{2,0},{4,6},{6,4},{8,10},{10,8},{12,14},{14,12},{16,18},{18,... | collective-permute-start | bytes 1474568 | tf_op jit(solution)/shard_map/ppermute | solution.py:446
  81.9 7.3 %collective-permute-start.25 = (bf16[1,600,128]{2,1,0:T(8,128)(2,1)S(1)}, bf16[1,600,128]{2,1,0:T(8,128)(2,1)S(1)}, u32[]{:S(2)}, u32[]{:S(2)}) collective-permute-start(bf16[1,600,128]{2,1,0:T(8,128)(2,1)S(1)} %get-tuple-element.72), channel_id=1, source_target_pairs={{0,1},{1,0},{2,3},{3,2},{4,5},{5,4},{6,7},{7,6},{8,9},{9,8},{10,11... | collective-permute-start | bytes 460808 | tf_op jit(solution)/shard_map/ppermute | solution.py:514
  85.8 6.4 %collective-permute-start.22 = (bf16[1,4,480,128]{3,2,1,0:T(8,128)(2,1)S(1)}, bf16[1,4,480,128]{3,2,1,0:T(8,128)(2,1)S(1)}, u32[]{:S(2)}, u32[]{:S(2)}) collective-permute-start(bf16[1,4,480,128]{3,2,1,0:T(8,128)(2,1)S(1)} %get-tuple-element.67.refs_2_), channel_id=1, source_target_pairs={{0,2},{2,0},{4,6},{6,4},{8,10},{10,8},{12,14},{14,12},{16,18},{18,... | collective-permute-start | bytes 1474568 | tf_op jit(solution)/shard_map/ppermute | solution.py:446
  86.7 7.5 %collective-permute-start.26 = (bf16[1,600,128]{2,1,0:T(8,128)(2,1)S(1)}, bf16[1,600,128]{2,1,0:T(8,128)(2,1)S(1)}, u32[]{:S(2)}, u32[]{:S(2)}) collective-permute-start(bf16[1,600,128]{2,1,0:T(8,128)(2,1)S(1)} %get-tuple-element.75), channel_id=1, source_target_pairs={{0,1},{1,0},{2,3},{3,2},{4,5},{5,4},{6,7},{7,6},{8,9},{9,8},{10,11... | collective-permute-start | bytes 460808 | tf_op jit(solution)/shard_map/ppermute | solution.py:514
  89.2 6.7 %collective-permute-start.30 = (bf16[2,2520,256]{2,1,0:T(8,128)(2,1)S(1)}, bf16[2,2520,256]{2,1,0:T(8,128)(2,1)S(1)}, u32[]{:S(2)}, u32[]{:S(2)}) collective-permute-start(bf16[2,2520,256]{2,1,0:T(8,128)(2,1)S(1)} %get-tuple-element.81), channel_id=1, source_target_pairs={{0,2},{2,0},{4,6},{6,4},{8,10},{10,8},{12,14},{14,12},{16,18},{18,... | collective-permute-start | bytes 7741448 | tf_op jit(solution)/shard_map/ppermute | solution.py:446
  91.6 3.3 %collective-permute-start.29 = (bf16[2,600,256]{2,1,0:T(8,128)(2,1)S(1)}, bf16[2,600,256]{2,1,0:T(8,128)(2,1)S(1)}, u32[]{:S(2)}, u32[]{:S(2)}) collective-permute-start(bf16[2,600,256]{2,1,0:T(8,128)(2,1)S(1)} %get-tuple-element.78), channel_id=1, source_target_pairs={{0,2},{2,0},{4,6},{6,4},{8,10},{10,8},{12,14},{14,12},{16,18},{18,... | collective-permute-start | bytes 1843208 | tf_op jit(solution)/shard_map/ppermute | solution.py:446
  94.3 1.4 %collective-permute-start.27 = (bf16[1,600,128]{2,1,0:T(8,128)(2,1)S(1)}, bf16[1,600,128]{2,1,0:T(8,128)(2,1)S(1)}, u32[]{:S(2)}, u32[]{:S(2)}) collective-permute-start(bf16[1,600,128]{2,1,0:T(8,128)(2,1)S(1)} %get-tuple-element.76.refs_0_), channel_id=1, source_target_pairs={{0,2},{2,0},{4,6},{6,4},{8,10},{10,8},{12,14},{14,12},{16,18},{18,... | collective-permute-start | bytes 460808 | tf_op jit(solution)/shard_map/ppermute | solution.py:446
  94.4 1.6 %collective-permute-start.28 = (bf16[1,600,128]{2,1,0:T(8,128)(2,1)S(1)}, bf16[1,600,128]{2,1,0:T(8,128)(2,1)S(1)}, u32[]{:S(2)}, u32[]{:S(2)}) collective-permute-start(bf16[1,600,128]{2,1,0:T(8,128)(2,1)S(1)} %get-tuple-element.77.refs_2_), channel_id=1, source_target_pairs={{0,2},{2,0},{4,6},{6,4},{8,10},{10,8},{12,14},{14,12},{16,18},{18,... | collective-permute-start | bytes 460808 | tf_op jit(solution)/shard_map/ppermute | solution.py:446
where the time goes:
time: 99.2 us; the launch traced here: 99.1 us
  waiting for transfers between devices  37.5 us (38%)
  starting transfers between devices  32.6 us (33%)
  Pallas kernels  25.9 us (26%)
  local copies, waits for them, and re-layouts  2.32 us (2%)
    ppermute x7, waiting for transfers between devices, do_extra(): across_came[d, 1 - part].append(lax.ppermute(extra, 'chan', across))  16.5 us
    ppermute x19, starting transfers between devices, permute_rows(): return [lax.ppermute(piece, 'rows', pairs) for piece in pieces]  16.3 us
    ppermute x19, waiting for transfers between devices, permute_rows(): return [lax.ppermute(piece, 'rows', pairs) for piece in pieces]  11.4 us
    ppermute x7, starting transfers between devices, do_extra(): across_came[d, 1 - part].append(lax.ppermute(extra, 'chan', across))  10.9 us
    pallas_call x3, Pallas kernels, correlate(): pl.pallas_call(functools.partial(corr_kernel, factor, tuple((len(part) fo...  9.09 us
    ppermute x1, waiting for transfers between devices, ring_local(): partner = lax.ppermute(theirs, 'chan', across)  7.99 us
    pallas_call x10, Pallas kernels, make_extra(): pl.pallas_call(functools.partial(extra_kernel, len(halves), 2 + len(carri...  7.39 us
    pallas_call x2, Pallas kernels, came_rows(): pl.pallas_call(functools.partial(came_kernel, factor, len(own), wide, len...  5.34 us
  transfers between devices with their start and end apart: 31, of which 18 were waited for; matrix products, arithmetic and copies ran while one was open for 1% of the time, Pallas kernels for 23%

commit v1 on v0

--- a/solution.py
+++ b/solution.py
@@ -8,7 +8,7 @@
 from jax.sharding import PartitionSpec as P
 
 LANES = 128
-PARAMS = {'LAG': 2, 'F0': 10, 'F1': 0, 'PS0': 2, 'JA': 1, 'JB': 1, 'C0POS': 2, 'R3POS': 0, 'GATE': 30, 'F3': 10, 'F2': 10, 'PE4': 1, 'X00': 10, 'X01': 10, 'C0': 10, 'X10': 10, 'X11': 10, 'C1': 10, 'X20': 10, 'X21': 10, 'C2': 10, 'X30': 10, 'X31': 10, 'C3': 10, 'X40': 10, 'X41': 10, 'C4': 10}
+PARAMS = {'LAG': 2, 'F0': 10, 'F1': 0, 'PS0': 2, 'JA': 1, 'JB': 1, 'C0POS': 2, 'R3POS': 0, 'GATE': 30, 'F3': 10, 'F2': 10, 'PE4': 0, 'X00': 10, 'X01': 10, 'C0': 10, 'X10': 10, 'X11': 10, 'C1': 10, 'X20': 10, 'X21': 10, 'C2': 10, 'X30': 10, 'X31': 10, 'C3': 10, 'X40': 10, 'X41': 10, 'C4': 10, 'NL': 1}
 
 
 def G(name):
@@ -177,13 +177,18 @@
     pass
 
 
-def raw_kernel(factor, arrays, wide, landing, meta, *refs):
+def first_open_row(total, raw):
+    return (2 * raw - total) // 16 * 16
+
+
+def raw_kernel(factor, arrays, wide, landing, leaving, slots, meta, *refs):
     own, other = strips_in(refs[:arrays]), strips_in(refs[arrays : 2 * arrays])
     queries, *refs = refs[2 * arrays :]
     landed = refs.pop(0) if landing else None
+    leavers, refs = refs[: len(leaving)], refs[len(leaving) :]
     _, out, done, *refs = refs
     pair = refs.pop(0) if wide else None
-    values, sums, sums_two, land_sems = refs
+    values, sums, sums_two, land_sems, sems = refs
     rows_n, cols_n, _ = own[0].shape
     count, width = done.shape[1] - rows_n * cols_n, done.shape[2]
     raw = rows_n * cols_n
@@ -193,6 +198,18 @@
     for index, slot in enumerate(landing):
         copies.append(pltpu.make_async_copy(landed.at[index], out.at[meta[slot]], land_sems.at[index]))
         copies[-1].start()
+    total, cut = done.shape[1], first_open_row(done.shape[1], rows_n * cols_n)
+    slots = list(slots)
+
+    def leave(strip, whole):
+        rows = pl.ds(0, total if whole else cut)
+        number = len(copies) - len(landing)
+        copies.append(pltpu.make_async_copy(strip.at[rows], out.at[meta[slots.pop(0)], rows], sems.at[number]))
+        copies[-1].start()
+
+    for strips, whole in zip(leavers, leaving):
+        for index in range(strips.shape[0]):
+            leave(strips.at[index], whole)
 
     def times(left):
         return jnp.dot(left, queries[...], preferred_element_type=jnp.float32) * factor
@@ -230,11 +247,13 @@
             for at, run in enumerate(chunks(segments, step)):
                 store(index, at * step, joined(run))
 
+        if slots:
+            leave(done.at[index], False)
     for copy in copies:
         copy.wait()
 
 
-def came_kernel(factor, arrays, wide, late, pins, slots, meta, *refs):
+def came_kernel(factor, arrays, wide, late, pins, slots, late_whole, meta, *refs):
     own, other = strips_in(refs[:arrays]), strips_in(refs[arrays : 2 * arrays])
     queries, *refs = refs[2 * arrays :]
     late_rows = refs.pop(0) if late else None
@@ -248,9 +267,13 @@
     ones = count * 4 // 5
     copies = []
 
-    def leave(strip):
-        copies.append(pltpu.make_async_copy(strip, out.at[meta[slots[len(copies)]]], sems.at[len(copies)]))
-        copies[-1].start()
+    def leave(strip, whole=False):
+        if slots:
+            cut = 0 if whole else first_open_row(raw + count, raw)
+            rows = pl.ds(cut, raw + count - cut)
+            slot = meta[slots[len(copies)]]
+            copies.append(pltpu.make_async_copy(strip.at[rows], out.at[slot, rows], sems.at[len(copies)]))
+            copies[-1].start()
 
     def merge(strip, part):
         @pl.when(meta[0] == 0)
@@ -275,7 +298,7 @@
     if late:
         for index in range(late_done.shape[0]):
             merge(late_done.at[index], late_rows[index].astype(jnp.float32))
-            leave(late_done.at[index])
+            leave(late_done.at[index], late_whole)
     for index, halves in enumerate(zip(own, other)):
         left = jnp.concatenate([half[...] for half in halves], axis=1)
         part = jnp.dot(left, queries[...], preferred_element_type=jnp.float32) * factor
@@ -333,18 +356,21 @@
         return pl.CostEstimate(flops=int(us * 10**9) + 1000, bytes_accessed=1000, transcendentals=0)
 
 
-    def make_extra(out, halves, cost=0, pins=(), flip=False, carry=False):
+    def make_extra(out, halves, cost=0, pins=(), flip=False, carry=False, passed=None):
         strips = sum(half.shape[0] for half in halves)
         handed = () if out is None else (out,)
         carried = tuple(halves) if carry else ()
         aliases = {1 + len(halves): 1} if handed else {}
         aliases.update({1 + index: 2 + index for index in range(len(carried))})
+        if passed is not None:
+            pins, carried = (passed, *pins), (passed,)
+            aliases[1 + len(halves) + len(handed)] = 2
         return pl.pallas_call(
             functools.partial(extra_kernel, len(halves), 2 + len(carried), flip),
             out_shape=(jax.ShapeDtypeStruct((strips, count, chans), frame_two.dtype), out_type)
             + tuple(jax.ShapeDtypeStruct(half.shape, half.dtype) for half in carried),
             in_specs=[scalars] + [in_vmem] * len(halves) + [anywhere] * len(handed + pins),
-            out_specs=(in_vmem, anywhere) + (in_vmem,) * len(carried),
+            out_specs=(in_vmem, anywhere) + (in_vmem if carry else anywhere,) * len(carried),
             scratch_shapes=pooling,
             input_output_aliases=aliases,
             compiler_params=params,
@@ -378,24 +404,27 @@
     def product_type(strips, pixels):
         return jax.ShapeDtypeStruct((strips, pixels, queries_n), frame_two.dtype)
 
-    def raw_rows(out, own, other, wide, landing=(), landed=None, cost=0):
+    def raw_rows(out, own, other, wide, landing=(), landed=None, cost=0, leavers=(), leaving=(), slots=(), pins=()):
         operands = [*own, *other, queries_wide if wide else queries]
         strips = sum(half.shape[0] for half in own)
+        passive = ([landed] if landing else []) + list(leavers)
+        pins = tuple(pins)
         return pl.pallas_call(
-            functools.partial(raw_kernel, factor, len(own), wide, landing),
+            functools.partial(raw_kernel, factor, len(own), wide, landing, leaving, slots),
             out_shape=(out_type,) + (product_type(strips, raw + count),) * (1 + wide),
-            in_specs=[scalars] + [in_vmem] * len(operands) + [anywhere] * (1 + bool(landing)),
+            in_specs=[scalars] + [in_vmem] * len(operands) + [anywhere] * (1 + len(passive)),
             out_specs=(anywhere,) + (in_vmem,) * (1 + wide),
             scratch_shapes=[
                 pltpu.VMEM((raw + count, queries_n * (1 + wide)), jnp.float32),
                 *pooling,
                 pltpu.SemaphoreType.DMA((max(1, len(landing)),)),
+                pltpu.SemaphoreType.DMA((max(1, len(slots)),)),
             ],
-            input_output_aliases={1 + len(operands) + bool(landing): 0},
+            input_output_aliases={1 + len(operands) + len(passive): 0},
             compiler_params=params,
             cost_estimate=modelled(cost),
             name="raw_rows",
-        )(meta, *operands, *([landed] if landing else []), out)
+        )(meta, *operands, *passive, out)
 
     def came_rows(out, done, slots, own, other, wide, late=(), cost=0, pins=()):
         operands = [*own, *other, queries_wide if wide else queries, *late[:1]]
@@ -403,13 +432,13 @@
         inout = [out, done, *late[1:]]
         extra_types = (product_type(done.shape[0], count),) if wide else ()
         return pl.pallas_call(
-            functools.partial(came_kernel, factor, len(own), wide, len(late) // 2, len(pins), slots),
+            functools.partial(came_kernel, factor, len(own), wide, len(late) // 2, len(pins), slots, not G("NL")),
             out_shape=tuple(jax.ShapeDtypeStruct(array.shape, array.dtype) for array in inout) + extra_types,
             in_specs=[scalars] + [in_vmem] * len(operands) + [anywhere] + [in_vmem] * (len(inout) - 1) + [anywhere] * len(pins),
             out_specs=(anywhere,) + (in_vmem,) * (len(inout) - 1 + wide),
             scratch_shapes=[
                 pltpu.VMEM((count, queries_n), jnp.float32),
-                pltpu.SemaphoreType.DMA((len(slots),)),
+                pltpu.SemaphoreType.DMA((max(1, len(slots)),)),
             ],
             input_output_aliases={first + index: index for index in range(len(inout))},
             compiler_params=params,
@@ -439,8 +468,11 @@
     else:
         partner = lax.ppermute(theirs, "chan", across)
         queries_other = lax.ppermute(frame_one, "chan", across)
-    queries = jnp.concatenate([frame_one.T, queries_other.T], axis=0)
-    queries_wide = jnp.concatenate([queries, lax.ppermute(queries, "rows", swap)], axis=1)
+    def all_queries(mine, theirs):
+        own_core = jnp.concatenate([mine.T, theirs.T], axis=0)
+        return own_core, jnp.concatenate([own_core, lax.ppermute(own_core, "rows", swap)], axis=1)
+
+    if not G("QC"): queries, queries_wide = all_queries(frame_one, queries_other)
 
     def permute_rows(pairs, pieces):
         return [lax.ppermute(piece, "rows", pairs) for piece in pieces]
@@ -456,9 +488,10 @@
             moving = [[pieces[0][:1]] for pieces in moving]
         if d == half_way - 1 and G("BSPL"):
             moving[1] = [moving[1][0][:1], moving[1][0][1:]]
-        moving = [
-            permute_rows(ring, whole(pieces) if d == join[part] else pieces) for part, pieces in enumerate(moving)
-        ]
+        moving = [whole(pieces) if d == join[part] else pieces for part, pieces in enumerate(moving)]
+        if d == 1:
+            ring_first = moving[1][-1]
+        moving = [permute_rows(ring, pieces) for pieces in moving]
         came[d] = tuple(moving)
     across_came = {}
 
@@ -485,7 +518,12 @@
         waiting.append((d + lag, slots_of(d, 1), permute_rows(swap, [pair])[0]))
         return out
 
-    out = do_extra(None, 0, 0, partner if G("PINX") else None)
+    if G("QC"):
+        extra, out, sent = make_extra(None, came[0][0], G("X00"), ({1: partner, 2: ring_first}[G("PINX")],) if G("PINX") else (), passed=frame_one)
+        across_came[0, 1] = [lax.ppermute(extra, "chan", across)]
+        queries, queries_wide = all_queries(frame_one, lax.ppermute(sent, "chan", across))
+    else:
+        out = do_extra(None, 0, 0, partner if G("PINX") else None)
     lacking, out = make_extra(out, [theirs], G("X01"), tuple(across_came[0, 1]) if G("PIN01") else (), flip=True)
     across_came[0, 0] = [lacking]
     if G("C0POS") == 0: out = product(out, 0)
@@ -520,20 +558,24 @@
     if R3 == 1: out, near_done, near_pair = near_raw(out)
     out = far_extra(out, 1, (swapped[0],) if G("PS0") == 1 else ())
     near_late = swap_one(near_pair)
-    pins = (tuple(across_came[far, 1]) if G("PE4") else ()) + ((swapped[0],) if G("PS0") == 2 else ())
-
-    def far_rows(out):
-        return raw_rows(out, [came[far][0][0], swapped[0]], [came[far][1][0], swapped[1]], False, *landing(far), G("F0"))
-
-    def near_came(out):
-        return came_rows(out, near_done, slots_of(near, 0), across_came[near, 0], across_came[near, 1], True, cost=G("F2"), pins=pins)
-
-    if G("FAR1"): out, far_done = far_rows(out)
-    out, _, near_rows = near_came(out)
+    pins = (tuple(across_came[far, 1]) if G("PE4") == 1 else ()) + ((swapped[0],) if G("PS0") == 2 else ())
+
+    slots = slots_of(near, 1) + slots_of(far, 0) + slots_of(far, 1)
+
+    out, near_done, near_rows = came_rows(out, near_done, (), across_came[near, 0], across_came[near, 1], True, cost=G("F2"), pins=pins)
     near_rows = swap_one(near_rows)
-    if not G("FAR1"): out, far_done = far_rows(out)
+    out, far_done = raw_rows(
+        out,
+        [came[far][0][0], swapped[0]],
+        [came[far][1][0], swapped[1]],
+        False,
+        *landing(far),
+        G("F0"),
+        (near_done, near_late) if G("NL") else (near_done,),
+        (True, False)[: 1 + G("NL")],
+        slots_of(near, 0) + (slots if G("NL") else slots[len(slots_of(near, 1)) :]),
+    )
     out, own, other = gate(out, [across_came[far, 0][0], across_came[far, 1][0]], G("GATE"))
-    slots = slots_of(near, 1) + slots_of(far, 0) + slots_of(far, 1)
     return came_rows(out, far_done, slots, [own, swap_one(own)], [other, swap_one(other)], False, (near_rows, near_late), G("F1"))[0]
 
 

time: 99.2 us -> 99.9 us (level)
  waiting for transfers between devices: 37.5 us -> 38.9 us
    pallas_call x2, Pallas kernels: 5.34 us -> 3.5 us  [came_rows(): pl.pallas_call(functools.partial(came_kernel, factor, len(own), wide, len...]
    ppermute x2, waiting for transfers between devices: 0.71 us -> 2.5 us  [far_extra(): across_came[far, 1 - part] = [lax.ppermute(extra, 'chan', across)]]
    pallas_call x2, Pallas kernels: 4.07 us -> 5.8 us  [raw_rows(): pl.pallas_call(functools.partial(raw_kernel, factor, len(own), wide, land...]
  transfers between devices with their start and end apart: 31 -> 31, of which waited for: 18 -> 16; matrix products, arithmetic and copies ran while one was open for 1% -> 1% of each run, Pallas kernels for 23% -> 24%
where the time goes in v1:
time: 99.9 us; the launch traced here: 99.7 us
  waiting for transfers between devices  38.9 us (39%)
  starting transfers between devices  32 us (32%)
  Pallas kernels  25.8 us (26%)
  local copies, waits for them, and re-layouts  2.32 us (2%)
    ppermute x19, starting transfers between devices, permute_rows(): return [lax.ppermute(piece, 'rows', pairs) for piece in pieces]  16.3 us
    ppermute x7, waiting for transfers between devices, do_extra(): across_came[d, 1 - part].append(lax.ppermute(extra, 'chan', across))  15.7 us
    ppermute x19, waiting for transfers between devices, permute_rows(): return [lax.ppermute(piece, 'rows', pairs) for piece in pieces]  11.8 us
    ppermute x7, starting transfers between devices, do_extra(): across_came[d, 1 - part].append(lax.ppermute(extra, 'chan', across))  10.9 us
    pallas_call x3, Pallas kernels, correlate(): pl.pallas_call(functools.partial(corr_kernel, factor, tuple((len(part) fo...  9.09 us
    ppermute x1, waiting for transfers between devices, ring_local(): partner = lax.ppermute(theirs, 'chan', across)  7.99 us
    pallas_call x10, Pallas kernels, make_extra(): pl.pallas_call(functools.partial(extra_kernel, len(halves), 2 + len(carri...  7.39 us
    pallas_call x2, Pallas kernels, raw_rows(): pl.pallas_call(functools.partial(raw_kernel, factor, len(own), wide, land...  5.8 us
  transfers between devices with their start and end apart: 31, of which 16 were waited for; matrix products, arithmetic and copies ran while one was open for 1% of the time, Pallas kernels for 24%

profile of v1, /device:TPU:0, one launch (start us, length us, event | category | flops | bytes accessed | tf_op | source)
XLA Modules:
  0.0 99.7 jit_solution(15759229416102886868)
XLA Ops:
  0.0 1.2 %dynamic-slice_bitcast_fusion = (bf16[1,4,480,128]{3,2,1,0:T(8,128)(2,1)S(1)}, bf16[1,4,480,128]{3,2,1,0:T(8,128)(2,1)S(1)}) fusion(bf16[8,480,128]{2,1,0:T(8,128)(2,1)} %param.3, s32[]{:T(128)S(6)} %select_n.72, s32[]{:T(128)S(6)} %select_n.71), kind=kLoop, calls=%fused_computation.2 | loop fusion | bytes 1966088 | tf_op jit(solution)/shard_map/broadcast_in_dim | solution.py:463
  1.8 2.6 %collective-permute-start.5 = (bf16[1,4,480,128]{3,2,1,0:T(8,128)(2,1)S(1)}, bf16[1,4,480,128]{3,2,1,0:T(8,128)(2,1)S(1)}, u32[]{:S(2)}, u32[]{:S(2)}) collective-permute-start(bf16[1,4,480,128]{3,2,1,0:T(8,128)(2,1)S(1)} %get-tuple-element.85.refs_0_), channel_id=1, source_target_pairs={{0,1},{1,0},{2,3},{3,2},{4,5},{5,4},{6,7},{7,6},{8,9},{9,8},{10,11... | collective-permute-start | bytes 1474568 | tf_op jit(solution)/shard_map/ppermute | solution.py:469
  4.3 0.9 copy.27
  6.3 2.1 %collective-permute-start.1 = (bf16[2,4,480,128]{3,2,1,0:T(8,128)(2,1)S(1)}, bf16[2,4,480,128]{3,2,1,0:T(8,128)(2,1)S(1)}, u32[]{:S(2)}, u32[]{:S(2)}) collective-permute-start(bf16[2,4,480,128]{3,2,1,0:T(8,128)(2,1)S(1)} %pad_maximum_fusion), channel_id=1, source_target_pairs={{0,8},{8,16},{16,24},{24,28},{28,20},{20,12},{12,4},{4,0},{2,6},{1... | collective-permute-start | bytes 2949128 | tf_op jit(solution)/shard_map/ppermute | solution.py:478
  8.4 8.0 %collective-permute-done.5.refs_1_ = bf16[1,4,480,128]{3,2,1,0:T(8,128)(2,1)S(1)} collective-permute-done((bf16[1,4,480,128]{3,2,1,0:T(8,128)(2,1)S(1)}, bf16[1,4,480,128]{3,2,1,0:T(8,128)(2,1)S(1)}, u32[]{:S(2)}, u32[]{:S(2)}) %collective-permute-start.5) | collective-permute-done | bytes 491552 | tf_op jit(solution)/shard_map/ppermute | solution.py:469
  17.0 1.3 %collective-permute-done.6 = bf16[1,4,480,128]{3,2,1,0:T(8,128)(2,1)S(1)} collective-permute-done((bf16[1,4,480,128]{3,2,1,0:T(8,128)(2,1)S(1)}, bf16[1,4,480,128]{3,2,1,0:T(8,128)(2,1)S(1)}, u32[]{:S(2)}, u32[]{:S(2)}) %collective-permute-start.6) | collective-permute-done | bytes 491552 | tf_op jit(solution)/shard_map/ppermute | solution.py:478
  18.4 2.1 %collective-permute-start.7 = (bf16[2,4,480,128]{3,2,1,0:T(8,128)(2,1)S(1)}, bf16[2,4,480,128]{3,2,1,0:T(8,128)(2,1)S(1)}, u32[]{:S(2)}, u32[]{:S(2)}) collective-permute-start(bf16[2,4,480,128]{3,2,1,0:T(8,128)(2,1)S(1)} %pad_maximum_fusion.1), channel_id=1, source_target_pairs={{0,8},{8,16},{16,24},{24,28},{28,20},{20,12},{12,4},{4,0},{2,6},{1... | collective-permute-start | bytes 2949128 | tf_op jit(solution)/shard_map/ppermute | solution.py:478
  20.5 0.8 extra.12
  21.2 1.8 %collective-permute-start.12 = (bf16[2,600,128]{2,1,0:T(8,128)(2,1)S(1)}, bf16[2,600,128]{2,1,0:T(8,128)(2,1)S(1)}, u32[]{:S(2)}, u32[]{:S(2)}) collective-permute-start(bf16[2,600,128]{2,1,0:T(8,128)(2,1)S(1)} %get-tuple-element.48), channel_id=1, source_target_pairs={{0,1},{1,0},{2,3},{3,2},{4,5},{5,4},{6,7},{7,6},{8,9},{9,8},{10,11... | collective-permute-start | bytes 921608 | tf_op jit(solution)/shard_map/ppermute | solution.py:504
  23.5 0.9 collective-permute-done.11
  24.5 1.6 %collective-permute-start.2 = (bf16[2,4,480,128]{3,2,1,0:T(8,128)(2,1)S(1)}, bf16[2,4,480,128]{3,2,1,0:T(8,128)(2,1)S(1)}, u32[]{:S(2)}, u32[]{:S(2)}) collective-permute-start(bf16[2,4,480,128]{3,2,1,0:T(8,128)(2,1)S(1)} %collective-permute-done.1.refs_0_), channel_id=1, source_target_pairs={{0,8},{8,16},{16,24},{24,28},{28,20},{20,12},{12,4},{4,0},{2,6},{1... | collective-permute-start | bytes 2949128 | tf_op jit(solution)/shard_map/ppermute | solution.py:478
  26.1 5.4 %collective-permute-done.12.refs_2_.refs_3_ = bf16[2,600,128]{2,1,0:T(8,128)(2,1)S(1)} collective-permute-done((bf16[2,600,128]{2,1,0:T(8,128)(2,1)S(1)}, bf16[2,600,128]{2,1,0:T(8,128)(2,1)S(1)}, u32[]{:S(2)}, u32[]{:S(2)}) %collective-permute-start.12) | collective-permute-done | bytes 307232 | tf_op jit(solution)/shard_map/ppermute | solution.py:504
  31.5 1.0 %collective-permute-done.7.refs_0_.refs_1_ = bf16[2,4,480,128]{3,2,1,0:T(8,128)(2,1)S(1)} collective-permute-done((bf16[2,4,480,128]{3,2,1,0:T(8,128)(2,1)S(1)}, bf16[2,4,480,128]{3,2,1,0:T(8,128)(2,1)S(1)}, u32[]{:S(2)}, u32[]{:S(2)}) %collective-permute-start.7) | collective-permute-done | bytes 983072 | tf_op jit(solution)/shard_map/ppermute | solution.py:478
  32.5 0.8 extra.13
  33.3 1.8 %collective-permute-start.13 = (bf16[2,600,128]{2,1,0:T(8,128)(2,1)S(1)}, bf16[2,600,128]{2,1,0:T(8,128)(2,1)S(1)}, u32[]{:S(2)}, u32[]{:S(2)}) collective-permute-start(bf16[2,600,128]{2,1,0:T(8,128)(2,1)S(1)} %get-tuple-element.49), channel_id=1, source_target_pairs={{0,1},{1,0},{2,3},{3,2},{4,5},{5,4},{6,7},{7,6},{8,9},{9,8},{10,11... | collective-permute-start | bytes 921608 | tf_op jit(solution)/shard_map/ppermute | solution.py:504
  35.1 2.5 %correlate.3 = (bf16[16,2520,256]{2,1,0:T(8,128)(2,1)}, bf16[1,2520,256]{2,1,0:T(8,128)(2,1)S(1)}) custom-call(s32[21]{0:T(128)S(1)} %concatenate.15.meta, bf16[1,4,480,128]{3,2,1,0:T(8,128)(2,1)S(1)} %get-tuple-element.86.refs_0_, bf16[1,4,480,128]{3,2,1,0:T(8,128)(2,1)S(1)} %collective-permute-done.5.refs_1_, ...), custom_call_target="tpu_custom_call", output_to_operand_aliasing={{0}: (6, {})} | custom-call | flops 10000001024 | bytes 1000 | tf_op jit(solution)/shard_map/correlate/pallas_call | solution.py:386
  37.7 1.6 %collective-permute-start.8 = (bf16[2,4,480,128]{3,2,1,0:T(8,128)(2,1)S(1)}, bf16[2,4,480,128]{3,2,1,0:T(8,128)(2,1)S(1)}, u32[]{:S(2)}, u32[]{:S(2)}) collective-permute-start(bf16[2,4,480,128]{3,2,1,0:T(8,128)(2,1)S(1)} %collective-permute-done.7.refs_0_.refs_1_), channel_id=1, source_target_pairs={{0,8},{8,16},{16,24},{24,28},{28,20},{20,12},{12,4},{4,0},{2,6},{1... | collective-permute-start | bytes 2949128 | tf_op jit(solution)/shard_map/ppermute | solution.py:478
  39.3 2.8 %collective-permute-done.13.refs_2_ = bf16[2,600,128]{2,1,0:T(8,128)(2,1)S(1)} collective-permute-done((bf16[2,600,128]{2,1,0:T(8,128)(2,1)S(1)}, bf16[2,600,128]{2,1,0:T(8,128)(2,1)S(1)}, u32[]{:S(2)}, u32[]{:S(2)}) %collective-permute-start.13) | collective-permute-done | bytes 307232 | tf_op jit(solution)/shard_map/ppermute | solution.py:504
  42.1 0.9 collective-permute-done.2.refs_0_
  43.0 0.8 extra.14
  43.8 1.8 %collective-permute-start.16 = (bf16[2,600,128]{2,1,0:T(8,128)(2,1)S(1)}, bf16[2,600,128]{2,1,0:T(8,128)(2,1)S(1)}, u32[]{:S(2)}, u32[]{:S(2)}) collective-permute-start(bf16[2,600,128]{2,1,0:T(8,128)(2,1)S(1)} %get-tuple-element.57), channel_id=1, source_target_pairs={{0,1},{1,0},{2,3},{3,2},{4,5},{5,4},{6,7},{7,6},{8,9},{9,8},{10,11... | collective-permute-start | bytes 921608 | tf_op jit(solution)/shard_map/ppermute | solution.py:504
  45.7 1.6 %collective-permute-start.3 = (bf16[2,4,480,128]{3,2,1,0:T(8,128)(2,1)S(1)}, bf16[2,4,480,128]{3,2,1,0:T(8,128)(2,1)S(1)}, u32[]{:S(2)}, u32[]{:S(2)}) collective-permute-start(bf16[2,4,480,128]{3,2,1,0:T(8,128)(2,1)S(1)} %collective-permute-done.2.refs_0_), channel_id=1, source_target_pairs={{0,8},{8,16},{16,24},{24,28},{28,20},{20,12},{12,4},{4,0},{2,6},{1... | collective-permute-start | bytes 2949128 | tf_op jit(solution)/shard_map/ppermute | solution.py:478
  47.2 3.3 %correlate.4 = (bf16[16,2520,256]{2,1,0:T(8,128)(2,1)}, bf16[2,2520,256]{2,1,0:T(8,128)(2,1)S(1)}) custom-call(s32[21]{0:T(128)S(1)} %concatenate.15.meta, bf16[2,4,480,128]{3,2,1,0:T(8,128)(2,1)S(1)} %collective-permute-done.1.refs_0_, bf16[2,4,480,128]{3,2,1,0:T(8,128)(2,1)S(1)} %collective-permute-done.7.refs_0_.refs_1_, ...), custom_call_target="tpu_custom_call", output_to_operand_aliasing={{0}: (6, {})} | custom-call | flops 10000001024 | bytes 1000 | tf_op jit(solution)/shard_map/correlate/pallas_call | solution.py:386
  50.6 2.1 %collective-permute-done.16.refs_2_.refs_3_ = bf16[2,600,128]{2,1,0:T(8,128)(2,1)S(1)} collective-permute-done((bf16[2,600,128]{2,1,0:T(8,128)(2,1)S(1)}, bf16[2,600,128]{2,1,0:T(8,128)(2,1)S(1)}, u32[]{:S(2)}, u32[]{:S(2)}) %collective-permute-start.16) | collective-permute-done | bytes 307232 | tf_op jit(solution)/shard_map/ppermute | solution.py:504
  52.6 0.9 collective-permute-done.8.refs_0_.refs_1_
  53.6 0.8 extra.15
  54.4 1.8 %collective-permute-start.17 = (bf16[2,600,128]{2,1,0:T(8,128)(2,1)S(1)}, bf16[2,600,128]{2,1,0:T(8,128)(2,1)S(1)}, u32[]{:S(2)}, u32[]{:S(2)}) collective-permute-start(bf16[2,600,128]{2,1,0:T(8,128)(2,1)S(1)} %get-tuple-element.58), channel_id=1, source_target_pairs={{0,1},{1,0},{2,3},{3,2},{4,5},{5,4},{6,7},{7,6},{8,9},{9,8},{10,11... | collective-permute-start | bytes 921608 | tf_op jit(solution)/shard_map/ppermute | solution.py:504
  56.2 1.6 %collective-permute-start.9 = (bf16[2,4,480,128]{3,2,1,0:T(8,128)(2,1)S(1)}, bf16[2,4,480,128]{3,2,1,0:T(8,128)(2,1)S(1)}, u32[]{:S(2)}, u32[]{:S(2)}) collective-permute-start(bf16[2,4,480,128]{3,2,1,0:T(8,128)(2,1)S(1)} %collective-permute-done.8.refs_0_.refs_1_), channel_id=1, source_target_pairs={{0,8},{8,16},{16,24},{24,28},{28,20},{20,12},{12,4},{4,0},{2,6},{1... | collective-permute-start | bytes 2949128 | tf_op jit(solution)/shard_map/ppermute | solution.py:478
  57.8 5.4 %collective-permute-done.17.refs_2_ = bf16[2,600,128]{2,1,0:T(8,128)(2,1)S(1)} collective-permute-done((bf16[2,600,128]{2,1,0:T(8,128)(2,1)S(1)}, bf16[2,600,128]{2,1,0:T(8,128)(2,1)S(1)}, u32[]{:S(2)}, u32[]{:S(2)}) %collective-permute-start.17) | collective-permute-done | bytes 307232 | tf_op jit(solution)/shard_map/ppermute | solution.py:504
  63.2 0.9 collective-permute-done.3.refs_0_
  64.1 0.8 extra.16
  64.9 1.8 %collective-permute-start.19 = (bf16[2,600,128]{2,1,0:T(8,128)(2,1)S(1)}, bf16[2,600,128]{2,1,0:T(8,128)(2,1)S(1)}, u32[]{:S(2)}, u32[]{:S(2)}) collective-permute-start(bf16[2,600,128]{2,1,0:T(8,128)(2,1)S(1)} %get-tuple-element.63), channel_id=1, source_target_pairs={{0,1},{1,0},{2,3},{3,2},{4,5},{5,4},{6,7},{7,6},{8,9},{9,8},{10,11... | collective-permute-start | bytes 921608 | tf_op jit(solution)/shard_map/ppermute | solution.py:504
  66.8 1.6 %collective-permute-start.4 = (bf16[1,4,480,128]{3,2,1,0:T(8,128)(2,1)S(1)}, bf16[1,4,480,128]{3,2,1,0:T(8,128)(2,1)S(1)}, u32[]{:S(2)}, u32[]{:S(2)}) collective-permute-start(bf16[1,4,480,128]{3,2,1,0:T(8,128)(2,1)S(1)} %slice.8), channel_id=1, source_target_pairs={{0,8},{8,16},{16,24},{24,28},{28,20},{20,12},{12,4},{4,0},{2,6},{1... | collective-permute-start | bytes 1474568 | tf_op jit(solution)/shard_map/ppermute | solution.py:478
  68.4 3.3 %correlate.5 = (bf16[16,2520,256]{2,1,0:T(8,128)(2,1)}, bf16[2,2520,256]{2,1,0:T(8,128)(2,1)S(1)}) custom-call(s32[21]{0:T(128)S(1)} %concatenate.15.meta, bf16[2,4,480,128]{3,2,1,0:T(8,128)(2,1)S(1)} %collective-permute-done.2.refs_0_, bf16[2,4,480,128]{3,2,1,0:T(8,128)(2,1)S(1)} %collective-permute-done.8.refs_0_.refs_1_, ...), custom_call_target="tpu_custom_call", output_to_operand_aliasing={{0}: (7, {})} | custom-call | flops 10000001024 | bytes 1000 | tf_op jit(solution)/shard_map/correlate/pallas_call | solution.py:386
  71.8 2.8 %collective-permute-done.9.refs_0_.refs_1_ = bf16[2,4,480,128]{3,2,1,0:T(8,128)(2,1)S(1)} collective-permute-done((bf16[2,4,480,128]{3,2,1,0:T(8,128)(2,1)S(1)}, bf16[2,4,480,128]{3,2,1,0:T(8,128)(2,1)S(1)}, u32[]{:S(2)}, u32[]{:S(2)}) %collective-permute-start.9) | collective-permute-done | bytes 983072 | tf_op jit(solution)/shard_map/ppermute | solution.py:478
  74.7 2.1 %collective-permute-start.21 = (bf16[1,4,480,128]{3,2,1,0:T(8,128)(2,1)S(1)}, bf16[1,4,480,128]{3,2,1,0:T(8,128)(2,1)S(1)}, u32[]{:S(2)}, u32[]{:S(2)}) collective-permute-start(bf16[1,4,480,128]{3,2,1,0:T(8,128)(2,1)S(1)} %slice.9), channel_id=1, source_target_pairs={{0,8},{8,16},{16,24},{24,28},{28,20},{20,12},{12,4},{4,0},{2,6},{1... | collective-permute-start | bytes 1474568 | tf_op jit(solution)/shard_map/ppermute | solution.py:478
  76.8 1.0 extra.17
  77.7 1.4 %collective-permute-start.24 = (bf16[2,600,128]{2,1,0:T(8,128)(2,1)S(1)}, bf16[2,600,128]{2,1,0:T(8,128)(2,1)S(1)}, u32[]{:S(2)}, u32[]{:S(2)}) collective-permute-start(bf16[2,600,128]{2,1,0:T(8,128)(2,1)S(1)} %get-tuple-element.70), channel_id=1, source_target_pairs={{0,1},{1,0},{2,3},{3,2},{4,5},{5,4},{6,7},{7,6},{8,9},{9,8},{10,11... | collective-permute-start | bytes 921608 | tf_op jit(solution)/shard_map/ppermute | solution.py:504
  79.1 2.0 %raw_rows.2 = (bf16[16,2520,256]{2,1,0:T(8,128)(2,1)}, bf16[2,2520,256]{2,1,0:T(8,128)(2,1)S(1)}, bf16[2,2520,256]{2,1,0:T(8,128)(2,1)S(1)}) custom-call(s32[21]{0:T(128)S(1)} %concatenate.15.meta, bf16[2,4,480,128]{3,2,1,0:T(8,128)(2,1)S(1)} %collective-permute-done.3.refs_0_, ...), custom_call_target="tpu_custom_call", output_to_operand_aliasing={{0}: (5, {})} | custom-call | flops 10000001024 | bytes 1000 | tf_op jit(solution)/shard_map/raw_rows/pallas_call | solution.py:412
  81.3 0.7 extra.18
  82.5 2.7 %collective-permute-done.21.refs_0_ = bf16[1,4,480,128]{3,2,1,0:T(8,128)(2,1)S(1)} collective-permute-done((bf16[1,4,480,128]{3,2,1,0:T(8,128)(2,1)S(1)}, bf16[1,4,480,128]{3,2,1,0:T(8,128)(2,1)S(1)}, u32[]{:S(2)}, u32[]{:S(2)}) %collective-permute-start.21) | collective-permute-done | bytes 491552 | tf_op jit(solution)/shard_map/ppermute | solution.py:478
  85.2 0.7 extra.19
  85.9 1.9 %collective-permute-start.26 = (bf16[1,600,128]{2,1,0:T(8,128)(2,1)S(1)}, bf16[1,600,128]{2,1,0:T(8,128)(2,1)S(1)}, u32[]{:S(2)}, u32[]{:S(2)}) collective-permute-start(bf16[1,600,128]{2,1,0:T(8,128)(2,1)S(1)} %get-tuple-element.77), channel_id=1, source_target_pairs={{0,1},{1,0},{2,3},{3,2},{4,5},{5,4},{6,7},{7,6},{8,9},{9,8},{10,11... | collective-permute-start | bytes 460808 | tf_op jit(solution)/shard_map/ppermute | solution.py:552
  88.0 1.3 %came_rows.2 = (bf16[16,2520,256]{2,1,0:T(8,128)(2,1)}, bf16[2,2520,256]{2,1,0:T(8,128)(2,1)S(1)}, bf16[2,600,256]{2,1,0:T(8,128)(2,1)S(1)}) custom-call(s32[21]{0:T(128)S(1)} %concatenate.15.meta, bf16[2,600,128]{2,1,0:T(8,128)(2,1)S(1)} %collective-permute-done.24.refs_0_, ...), custom_call_target="tpu_custom_call", output_to_operand_aliasing={{0}: (4, {}), {1}: (5, {})} | custom-call | flops 10000001024 | bytes 1000 | tf_op jit(solution)/shard_map/came_rows/pallas_call | solution.py:434
  89.4 3.8 %raw_rows.3 = (bf16[16,2520,256]{2,1,0:T(8,128)(2,1)}, bf16[2,2520,256]{2,1,0:T(8,128)(2,1)S(1)}) custom-call(s32[21]{0:T(128)S(1)} %concatenate.15.meta, bf16[1,4,480,128]{3,2,1,0:T(8,128)(2,1)S(1)} %get-tuple-element.66.refs_0_, bf16[1,4,480,128]{3,2,1,0:T(8,128)(2,1)S(1)} %collective-permute-done.20.refs_5_.refs_1_, ...), custom_call_target="tpu_custom_call", output_to_operand_aliasing={{0}: (9, {})} | custom-call | flops 10000001024 | bytes 1000 | tf_op jit(solution)/shard_map/raw_rows/pallas_call | solution.py:412
  93.2 2.5 %collective-permute-done.27.refs_2_ = bf16[1,600,128]{2,1,0:T(8,128)(2,1)S(1)} collective-permute-done((bf16[1,600,128]{2,1,0:T(8,128)(2,1)S(1)}, bf16[1,600,128]{2,1,0:T(8,128)(2,1)S(1)}, u32[]{:S(2)}, u32[]{:S(2)}) %collective-permute-start.27) | collective-permute-done | bytes 153632 | tf_op jit(solution)/shard_map/ppermute | solution.py:552
  96.2 0.9 collective-permute-done.28.refs_1_
  97.3 2.2 %came_rows.3 = (bf16[16,2520,256]{2,1,0:T(8,128)(2,1)}, bf16[2,2520,256]{2,1,0:T(8,128)(2,1)S(1)}, bf16[2,2520,256]{2,1,0:T(8,128)(2,1)S(1)}) custom-call(s32[21]{0:T(128)S(1)} %concatenate.15.meta, bf16[1,600,128]{2,1,0:T(8,128)(2,1)S(1)} %get-tuple-element.79.refs_0_, ...), custom_call_target="tpu_custom_call", output_to_operand_aliasing={{0}: (7, {}), {1}: (8, {}), {2}: (9, {})} | custom-call | flops 1000 | bytes 1000 | tf_op jit(solution)/shard_map/came_rows/pallas_call | solution.py:434
  (43 shorter events, 4.6 us)
Async XLA Ops:
  1.2 5.0 %collective-permute-start = (bf16[1,4,480,128]{3,2,1,0:T(8,128)(2,1)S(1)}, bf16[1,4,480,128]{3,2,1,0:T(8,128)(2,1)S(1)}, u32[]{:S(2)}, u32[]{:S(2)}) collective-permute-start(bf16[1,4,480,128]{3,2,1,0:T(8,128)(2,1)S(1)} %get-tuple-element.86.refs_0_), channel_id=1, source_target_pairs={{0,2},{2,0},{4,6},{6,4},{8,10},{10,8},{12,14},{14,12},{16,18},{18,... | collective-permute-start | bytes 1474568 | tf_op jit(solution)/shard_map/ppermute | solution.py:478
  1.8 14.6 %collective-permute-start.5 = (bf16[1,4,480,128]{3,2,1,0:T(8,128)(2,1)S(1)}, bf16[1,4,480,128]{3,2,1,0:T(8,128)(2,1)S(1)}, u32[]{:S(2)}, u32[]{:S(2)}) collective-permute-start(bf16[1,4,480,128]{3,2,1,0:T(8,128)(2,1)S(1)} %get-tuple-element.85.refs_0_), channel_id=1, source_target_pairs={{0,1},{1,0},{2,3},{3,2},{4,5},{5,4},{6,7},{7,6},{8,9},{9,8},{10,11... | collective-permute-start | bytes 1474568 | tf_op jit(solution)/shard_map/ppermute | solution.py:469
  5.3 17.7 %collective-permute-start.10 = (bf16[256,128]{0,1:T(8,128)(2,1)S(1)}, bf16[256,128]{0,1:T(8,128)(2,1)S(1)}, u32[]{:S(2)}, u32[]{:S(2)}) collective-permute-start(bf16[256,128]{0,1:T(8,128)(2,1)S(1)} %copy.27), channel_id=1, source_target_pairs={{0,1},{1,0},{2,3},{3,2},{4,5},{5,4},{6,7},{7,6},{8,9},{9,8},{10,11... | collective-permute-start | bytes 196616 | tf_op jit(solution)/shard_map/ppermute | solution.py:470
  6.3 14.1 %collective-permute-start.1 = (bf16[2,4,480,128]{3,2,1,0:T(8,128)(2,1)S(1)}, bf16[2,4,480,128]{3,2,1,0:T(8,128)(2,1)S(1)}, u32[]{:S(2)}, u32[]{:S(2)}) collective-permute-start(bf16[2,4,480,128]{3,2,1,0:T(8,128)(2,1)S(1)} %pad_maximum_fusion), channel_id=1, source_target_pairs={{0,8},{8,16},{16,24},{24,28},{28,20},{20,12},{12,4},{4,0},{2,6},{1... | collective-permute-start | bytes 2949128 | tf_op jit(solution)/shard_map/ppermute | solution.py:478
  16.4 1.9 %collective-permute-start.6 = (bf16[1,4,480,128]{3,2,1,0:T(8,128)(2,1)S(1)}, bf16[1,4,480,128]{3,2,1,0:T(8,128)(2,1)S(1)}, u32[]{:S(2)}, u32[]{:S(2)}) collective-permute-start(bf16[1,4,480,128]{3,2,1,0:T(8,128)(2,1)S(1)} %collective-permute-done.5.refs_1_), channel_id=1, source_target_pairs={{0,2},{2,0},{4,6},{6,4},{8,10},{10,8},{12,14},{14,12},{16,18},{18,... | collective-permute-start | bytes 1474568 | tf_op jit(solution)/shard_map/ppermute | solution.py:478
  18.4 14.1 %collective-permute-start.7 = (bf16[2,4,480,128]{3,2,1,0:T(8,128)(2,1)S(1)}, bf16[2,4,480,128]{3,2,1,0:T(8,128)(2,1)S(1)}, u32[]{:S(2)}, u32[]{:S(2)}) collective-permute-start(bf16[2,4,480,128]{3,2,1,0:T(8,128)(2,1)S(1)} %pad_maximum_fusion.1), channel_id=1, source_target_pairs={{0,8},{8,16},{16,24},{24,28},{28,20},{20,12},{12,4},{4,0},{2,6},{1... | collective-permute-start | bytes 2949128 | tf_op jit(solution)/shard_map/ppermute | solution.py:478
  21.2 10.2 %collective-permute-start.12 = (bf16[2,600,128]{2,1,0:T(8,128)(2,1)S(1)}, bf16[2,600,128]{2,1,0:T(8,128)(2,1)S(1)}, u32[]{:S(2)}, u32[]{:S(2)}) collective-permute-start(bf16[2,600,128]{2,1,0:T(8,128)(2,1)S(1)} %get-tuple-element.48), channel_id=1, source_target_pairs={{0,1},{1,0},{2,3},{3,2},{4,5},{5,4},{6,7},{7,6},{8,9},{9,8},{10,11... | collective-permute-start | bytes 921608 | tf_op jit(solution)/shard_map/ppermute | solution.py:504
  23.0 1.4 %collective-permute-start.11 = (bf16[256,256]{1,0:T(8,128)(2,1)S(1)}, bf16[256,256]{1,0:T(8,128)(2,1)S(1)}, u32[]{:S(2)}, u32[]{:S(2)}) collective-permute-start(bf16[256,256]{1,0:T(8,128)(2,1)S(1)} %pad_maximum_fusion.3.refs_4_), channel_id=1, source_target_pairs={{0,2},{2,0},{4,6},{6,4},{8,10},{10,8},{12,14},{14,12},{16,18},{18,... | collective-permute-start | bytes 393224 | tf_op jit(solution)/shard_map/ppermute | solution.py:473
  23.1 12.0 %collective-permute-start.14 = (bf16[1,600,128]{2,1,0:T(8,128)(2,1)S(1)}, bf16[1,600,128]{2,1,0:T(8,128)(2,1)S(1)}, u32[]{:S(2)}, u32[]{:S(2)}) collective-permute-start(bf16[1,600,128]{2,1,0:T(8,128)(2,1)S(1)} %get-tuple-element.51), channel_id=1, source_target_pairs={{0,1},{1,0},{2,3},{3,2},{4,5},{5,4},{6,7},{7,6},{8,9},{9,8},{10,11... | collective-permute-start | bytes 460808 | tf_op jit(solution)/shard_map/ppermute | solution.py:504
  24.5 18.6 %collective-permute-start.2 = (bf16[2,4,480,128]{3,2,1,0:T(8,128)(2,1)S(1)}, bf16[2,4,480,128]{3,2,1,0:T(8,128)(2,1)S(1)}, u32[]{:S(2)}, u32[]{:S(2)}) collective-permute-start(bf16[2,4,480,128]{3,2,1,0:T(8,128)(2,1)S(1)} %collective-permute-done.1.refs_0_), channel_id=1, source_target_pairs={{0,8},{8,16},{16,24},{24,28},{28,20},{20,12},{12,4},{4,0},{2,6},{1... | collective-permute-start | bytes 2949128 | tf_op jit(solution)/shard_map/ppermute | solution.py:478
  33.3 8.8 %collective-permute-start.13 = (bf16[2,600,128]{2,1,0:T(8,128)(2,1)S(1)}, bf16[2,600,128]{2,1,0:T(8,128)(2,1)S(1)}, u32[]{:S(2)}, u32[]{:S(2)}) collective-permute-start(bf16[2,600,128]{2,1,0:T(8,128)(2,1)S(1)} %get-tuple-element.49), channel_id=1, source_target_pairs={{0,1},{1,0},{2,3},{3,2},{4,5},{5,4},{6,7},{7,6},{8,9},{9,8},{10,11... | collective-permute-start | bytes 921608 | tf_op jit(solution)/shard_map/ppermute | solution.py:504
  37.6 30.8 %collective-permute-start.18 = (bf16[1,2520,256]{2,1,0:T(8,128)(2,1)S(1)}, bf16[1,2520,256]{2,1,0:T(8,128)(2,1)S(1)}, u32[]{:S(2)}, u32[]{:S(2)}) collective-permute-start(bf16[1,2520,256]{2,1,0:T(8,128)(2,1)S(1)} %get-tuple-element.59), channel_id=1, source_target_pairs={{0,2},{2,0},{4,6},{6,4},{8,10},{10,8},{12,14},{14,12},{16,18},{18,... | collective-permute-start | bytes 3870728 | tf_op jit(solution)/shard_map/ppermute | solution.py:478
  37.7 15.9 %collective-permute-start.8 = (bf16[2,4,480,128]{3,2,1,0:T(8,128)(2,1)S(1)}, bf16[2,4,480,128]{3,2,1,0:T(8,128)(2,1)S(1)}, u32[]{:S(2)}, u32[]{:S(2)}) collective-permute-start(bf16[2,4,480,128]{3,2,1,0:T(8,128)(2,1)S(1)} %collective-permute-done.7.refs_0_.refs_1_), channel_id=1, source_target_pairs={{0,8},{8,16},{16,24},{24,28},{28,20},{20,12},{12,4},{4,0},{2,6},{1... | collective-permute-start | bytes 2949128 | tf_op jit(solution)/shard_map/ppermute | solution.py:478
  43.8 8.8 %collective-permute-start.16 = (bf16[2,600,128]{2,1,0:T(8,128)(2,1)S(1)}, bf16[2,600,128]{2,1,0:T(8,128)(2,1)S(1)}, u32[]{:S(2)}, u32[]{:S(2)}) collective-permute-start(bf16[2,600,128]{2,1,0:T(8,128)(2,1)S(1)} %get-tuple-element.57), channel_id=1, source_target_pairs={{0,1},{1,0},{2,3},{3,2},{4,5},{5,4},{6,7},{7,6},{8,9},{9,8},{10,11... | collective-permute-start | bytes 921608 | tf_op jit(solution)/shard_map/ppermute | solution.py:504
  45.7 18.4 %collective-permute-start.3 = (bf16[2,4,480,128]{3,2,1,0:T(8,128)(2,1)S(1)}, bf16[2,4,480,128]{3,2,1,0:T(8,128)(2,1)S(1)}, u32[]{:S(2)}, u32[]{:S(2)}) collective-permute-start(bf16[2,4,480,128]{3,2,1,0:T(8,128)(2,1)S(1)} %collective-permute-done.2.refs_0_), channel_id=1, source_target_pairs={{0,8},{8,16},{16,24},{24,28},{28,20},{20,12},{12,4},{4,0},{2,6},{1... | collective-permute-start | bytes 2949128 | tf_op jit(solution)/shard_map/ppermute | solution.py:478
  54.4 8.8 %collective-permute-start.17 = (bf16[2,600,128]{2,1,0:T(8,128)(2,1)S(1)}, bf16[2,600,128]{2,1,0:T(8,128)(2,1)S(1)}, u32[]{:S(2)}, u32[]{:S(2)}) collective-permute-start(bf16[2,600,128]{2,1,0:T(8,128)(2,1)S(1)} %get-tuple-element.58), channel_id=1, source_target_pairs={{0,1},{1,0},{2,3},{3,2},{4,5},{5,4},{6,7},{7,6},{8,9},{9,8},{10,11... | collective-permute-start | bytes 921608 | tf_op jit(solution)/shard_map/ppermute | solution.py:504
  56.2 22.9 %collective-permute-start.15 = (bf16[2,2520,256]{2,1,0:T(8,128)(2,1)S(1)}, bf16[2,2520,256]{2,1,0:T(8,128)(2,1)S(1)}, u32[]{:S(2)}, u32[]{:S(2)}) collective-permute-start(bf16[2,2520,256]{2,1,0:T(8,128)(2,1)S(1)} %get-tuple-element.55), channel_id=1, source_target_pairs={{0,2},{2,0},{4,6},{6,4},{8,10},{10,8},{12,14},{14,12},{16,18},{18,... | collective-permute-start | bytes 7741448 | tf_op jit(solution)/shard_map/ppermute | solution.py:478
  56.2 18.4 %collective-permute-start.9 = (bf16[2,4,480,128]{3,2,1,0:T(8,128)(2,1)S(1)}, bf16[2,4,480,128]{3,2,1,0:T(8,128)(2,1)S(1)}, u32[]{:S(2)}, u32[]{:S(2)}) collective-permute-start(bf16[2,4,480,128]{3,2,1,0:T(8,128)(2,1)S(1)} %collective-permute-done.8.refs_0_.refs_1_), channel_id=1, source_target_pairs={{0,8},{8,16},{16,24},{24,28},{28,20},{20,12},{12,4},{4,0},{2,6},{1... | collective-permute-start | bytes 2949128 | tf_op jit(solution)/shard_map/ppermute | solution.py:478
  64.9 11.9 %collective-permute-start.19 = (bf16[2,600,128]{2,1,0:T(8,128)(2,1)S(1)}, bf16[2,600,128]{2,1,0:T(8,128)(2,1)S(1)}, u32[]{:S(2)}, u32[]{:S(2)}) collective-permute-start(bf16[2,600,128]{2,1,0:T(8,128)(2,1)S(1)} %get-tuple-element.63), channel_id=1, source_target_pairs={{0,1},{1,0},{2,3},{3,2},{4,5},{5,4},{6,7},{7,6},{8,9},{9,8},{10,11... | collective-permute-start | bytes 921608 | tf_op jit(solution)/shard_map/ppermute | solution.py:504
  66.8 14.5 %collective-permute-start.4 = (bf16[1,4,480,128]{3,2,1,0:T(8,128)(2,1)S(1)}, bf16[1,4,480,128]{3,2,1,0:T(8,128)(2,1)S(1)}, u32[]{:S(2)}, u32[]{:S(2)}) collective-permute-start(bf16[1,4,480,128]{3,2,1,0:T(8,128)(2,1)S(1)} %slice.8), channel_id=1, source_target_pairs={{0,8},{8,16},{16,24},{24,28},{28,20},{20,12},{12,4},{4,0},{2,6},{1... | collective-permute-start | bytes 1474568 | tf_op jit(solution)/shard_map/ppermute | solution.py:478
  71.7 17.7 %collective-permute-start.23 = (bf16[2,2520,256]{2,1,0:T(8,128)(2,1)S(1)}, bf16[2,2520,256]{2,1,0:T(8,128)(2,1)S(1)}, u32[]{:S(2)}, u32[]{:S(2)}) collective-permute-start(bf16[2,2520,256]{2,1,0:T(8,128)(2,1)S(1)} %get-tuple-element.69), channel_id=1, source_target_pairs={{0,2},{2,0},{4,6},{6,4},{8,10},{10,8},{12,14},{14,12},{16,18},{18,... | collective-permute-start | bytes 7741448 | tf_op jit(solution)/shard_map/ppermute | solution.py:478
  74.7 10.5 %collective-permute-start.21 = (bf16[1,4,480,128]{3,2,1,0:T(8,128)(2,1)S(1)}, bf16[1,4,480,128]{3,2,1,0:T(8,128)(2,1)S(1)}, u32[]{:S(2)}, u32[]{:S(2)}) collective-permute-start(bf16[1,4,480,128]{3,2,1,0:T(8,128)(2,1)S(1)} %slice.9), channel_id=1, source_target_pairs={{0,8},{8,16},{16,24},{24,28},{28,20},{20,12},{12,4},{4,0},{2,6},{1... | collective-permute-start | bytes 1474568 | tf_op jit(solution)/shard_map/ppermute | solution.py:478
  77.7 8.2 %collective-permute-start.24 = (bf16[2,600,128]{2,1,0:T(8,128)(2,1)S(1)}, bf16[2,600,128]{2,1,0:T(8,128)(2,1)S(1)}, u32[]{:S(2)}, u32[]{:S(2)}) collective-permute-start(bf16[2,600,128]{2,1,0:T(8,128)(2,1)S(1)} %get-tuple-element.70), channel_id=1, source_target_pairs={{0,1},{1,0},{2,3},{3,2},{4,5},{5,4},{6,7},{7,6},{8,9},{9,8},{10,11... | collective-permute-start | bytes 921608 | tf_op jit(solution)/shard_map/ppermute | solution.py:504
  81.2 8.3 %collective-permute-start.25 = (bf16[2,2520,256]{2,1,0:T(8,128)(2,1)S(1)}, bf16[2,2520,256]{2,1,0:T(8,128)(2,1)S(1)}, u32[]{:S(2)}, u32[]{:S(2)}) collective-permute-start(bf16[2,2520,256]{2,1,0:T(8,128)(2,1)S(1)} %get-tuple-element.74), channel_id=1, source_target_pairs={{0,2},{2,0},{4,6},{6,4},{8,10},{10,8},{12,14},{14,12},{16,18},{18,... | collective-permute-start | bytes 7741448 | tf_op jit(solution)/shard_map/ppermute | solution.py:478
  81.9 5.9 %collective-permute-start.20 = (bf16[1,4,480,128]{3,2,1,0:T(8,128)(2,1)S(1)}, bf16[1,4,480,128]{3,2,1,0:T(8,128)(2,1)S(1)}, u32[]{:S(2)}, u32[]{:S(2)}) collective-permute-start(bf16[1,4,480,128]{3,2,1,0:T(8,128)(2,1)S(1)} %get-tuple-element.66.refs_0_), channel_id=1, source_target_pairs={{0,2},{2,0},{4,6},{6,4},{8,10},{10,8},{12,14},{14,12},{16,18},{18,... | collective-permute-start | bytes 1474568 | tf_op jit(solution)/shard_map/ppermute | solution.py:478
  85.8 3.5 %collective-permute-start.22 = (bf16[1,4,480,128]{3,2,1,0:T(8,128)(2,1)S(1)}, bf16[1,4,480,128]{3,2,1,0:T(8,128)(2,1)S(1)}, u32[]{:S(2)}, u32[]{:S(2)}) collective-permute-start(bf16[1,4,480,128]{3,2,1,0:T(8,128)(2,1)S(1)} %get-tuple-element.68.refs_2_), channel_id=1, source_target_pairs={{0,2},{2,0},{4,6},{6,4},{8,10},{10,8},{12,14},{14,12},{16,18},{18,... | collective-permute-start | bytes 1474568 | tf_op jit(solution)/shard_map/ppermute | solution.py:478
  85.9 7.3 %collective-permute-start.26 = (bf16[1,600,128]{2,1,0:T(8,128)(2,1)S(1)}, bf16[1,600,128]{2,1,0:T(8,128)(2,1)S(1)}, u32[]{:S(2)}, u32[]{:S(2)}) collective-permute-start(bf16[1,600,128]{2,1,0:T(8,128)(2,1)S(1)} %get-tuple-element.77), channel_id=1, source_target_pairs={{0,1},{1,0},{2,3},{3,2},{4,5},{5,4},{6,7},{7,6},{8,9},{9,8},{10,11... | collective-permute-start | bytes 460808 | tf_op jit(solution)/shard_map/ppermute | solution.py:552
  87.9 7.9 %collective-permute-start.27 = (bf16[1,600,128]{2,1,0:T(8,128)(2,1)S(1)}, bf16[1,600,128]{2,1,0:T(8,128)(2,1)S(1)}, u32[]{:S(2)}, u32[]{:S(2)}) collective-permute-start(bf16[1,600,128]{2,1,0:T(8,128)(2,1)S(1)} %get-tuple-element.78), channel_id=1, source_target_pairs={{0,1},{1,0},{2,3},{3,2},{4,5},{5,4},{6,7},{7,6},{8,9},{9,8},{10,11... | collective-permute-start | bytes 460808 | tf_op jit(solution)/shard_map/ppermute | solution.py:552
  89.3 6.9 %collective-permute-start.30 = (bf16[2,600,256]{2,1,0:T(8,128)(2,1)S(1)}, bf16[2,600,256]{2,1,0:T(8,128)(2,1)S(1)}, u32[]{:S(2)}, u32[]{:S(2)}) collective-permute-start(bf16[2,600,256]{2,1,0:T(8,128)(2,1)S(1)} %get-tuple-element.81), channel_id=1, source_target_pairs={{0,2},{2,0},{4,6},{6,4},{8,10},{10,8},{12,14},{14,12},{16,18},{18,... | collective-permute-start | bytes 1843208 | tf_op jit(solution)/shard_map/ppermute | solution.py:478
  95.7 1.4 %collective-permute-start.28 = (bf16[1,600,128]{2,1,0:T(8,128)(2,1)S(1)}, bf16[1,600,128]{2,1,0:T(8,128)(2,1)S(1)}, u32[]{:S(2)}, u32[]{:S(2)}) collective-permute-start(bf16[1,600,128]{2,1,0:T(8,128)(2,1)S(1)} %get-tuple-element.79.refs_0_), channel_id=1, source_target_pairs={{0,2},{2,0},{4,6},{6,4},{8,10},{10,8},{12,14},{14,12},{16,18},{18,... | collective-permute-start | bytes 460808 | tf_op jit(solution)/shard_map/ppermute | solution.py:478
  95.7 1.6 %collective-permute-start.29 = (bf16[1,600,128]{2,1,0:T(8,128)(2,1)S(1)}, bf16[1,600,128]{2,1,0:T(8,128)(2,1)S(1)}, u32[]{:S(2)}, u32[]{:S(2)}) collective-permute-start(bf16[1,600,128]{2,1,0:T(8,128)(2,1)S(1)} %get-tuple-element.80.refs_2_), channel_id=1, source_target_pairs={{0,2},{2,0},{4,6},{6,4},{8,10},{10,8},{12,14},{14,12},{16,18},{18,... | collective-permute-start | bytes 460808 | tf_op jit(solution)/shard_map/ppermute | solution.py:478
